TPU v7x, 32 devices: a whole 2x2x4 slice. The times are simulated.
32 devices in a mesh: box: 8 (over z, x), dir: 4 (over y, core).
Axes of the slice: x: 2, y: 2, z: 4, core: 2. Of those that a mesh axis runs over, the one named last changes fastest.
Arguments:
- fine_out: bfloat16 [512, 32, 512], P(('box', 'dir')), may hold values from -6 to 6
- fine_list: int32 [512, 12], P(('box', 'dir')), may hold values from -1 to 511, as said below
- fine_slot: int32 [512], P('box'), may hold values from 0 to 3, as said below
- fine_translator: float32 [12, 2, 512], replicated, may hold values from -4 to 4
- theta_up_fine: bfloat16 [32, 16], replicated, may hold values from -1.5 to 1.5
- phi_up_fine: bfloat16 [64, 32], replicated, may hold values from -1 to 1
- middle_phase: float32 [4, 2048], replicated, may hold values from -3.140625 to 3.140625
- middle_list: int32 [128, 12], P('box'), may hold values from -1 to 127, as said below
- middle_slot: int32 [128], P('box'), may hold values from 0 to 3, as said below
- middle_translator: float32 [12, 2, 2048], P(None, None, 'dir'), may hold values from -2 to 2
- theta_up_middle: bfloat16 [64, 32], replicated, may hold values from -1 to 1
- phi_up_middle: bfloat16 [128, 64], replicated, may hold values from -0.75 to 0.75
- coarse_phase: float32 [4, 8192], replicated, may hold values from -3.140625 to 3.140625
- coarse_list: int32 [32, 12], replicated, may hold values from -1 to 31, as said below
- coarse_translator: float32 [12, 2, 8192], P(None, None, ('box', 'dir')), may hold values from -1.25 to 1.25
Outputs:
- fine_in: bfloat16 [512, 32, 512], P(('box', 'dir'))
- middle_in: bfloat16 [128, 32, 2048], P('box', None, 'dir')
- coarse_in: bfloat16 [32, 32, 8192], P(None, None, ('box', 'dir'))
Inputs may be any that keep to these rules, and one draw needn't show every extreme that they name: `fine_list`: row i names distinct fine boxes j with 2 <= |j - i| <= 7 and |j // 4 - i // 4| <= 1, in any slots; -1 marks an empty slot. `middle_list`: row i names distinct middle boxes j with 2 <= |j - i| <= 7 and |j // 4 - i // 4| <= 1, in any slots; -1 marks an empty slot. `coarse_list`: row i names distinct coarse boxes j with 2 <= |j - i| <= 7 and |j // 4 - i // 4| <= 1, in any slots; -1 marks an empty slot. `fine_slot`: the parent of fine box c is middle box c // 4; each aligned group of 4 fine boxes takes each of the values 0 to 3 once. `middle_slot`: the parent of middle box m is coarse box m // 4; each aligned group of 4 middle boxes takes each of the values 0 to 3 once.
All inputs are finite; a program needn't handle non-finite values.
Results may differ from a plain program's by a relative error of at most 0.007.
Values may be sent and summed in bfloat16 or wider, within the bound.
A program may use at most 64 MiB of HBM per device.

v0:
```python
import jax
import jax.numpy as jnp
from jax import lax
from jax.sharding import PartitionSpec as P

MAX_OFFSET = 7


def padded_2(cells, sides, width):
    for axis, dim in sides:
        count = lax.axis_size(axis)
        ends = count - 1
        head = lax.slice_in_dim(cells, 0, width, axis=dim)
        tail = lax.slice_in_dim(cells, cells.shape[dim] - width, cells.shape[dim], axis=dim)
        cells = jnp.concatenate(
            [
                lax.ppermute(tail, axis, [(i, (i + 1) % count) for i in range(ends)]),
                cells,
                lax.ppermute(head, axis, [((i + 1) % count, i) for i in range(ends)]),
            ],
            axis=dim,
        )
    return cells


def split_times(real_part, imag_part, pattern_real, pattern_imag):
    return (
        real_part * pattern_real - imag_part * pattern_imag,
        real_part * pattern_imag + imag_part * pattern_real,
    )


def offsets_used():
    return list(range(-MAX_OFFSET, -1)) + list(range(2, MAX_OFFSET + 1))


def translate_rows(padded, entries, first_box, translator):
    row_count = entries.shape[0]
    half_size = padded.shape[1] // 2
    box_ids = first_box + jnp.arange(row_count, dtype=jnp.int32)
    real_sum = jnp.zeros((row_count, half_size, padded.shape[2]), jnp.float32)
    imag_sum = jnp.zeros((row_count, half_size, padded.shape[2]), jnp.float32)
    for slot_index, offset in enumerate(offsets_used()):
        present = jnp.any(entries == (box_ids + offset)[:, None], axis=1).astype(jnp.float32)[
            :, None, None
        ]
        source = padded[MAX_OFFSET + offset : MAX_OFFSET + offset + row_count]
        real_term, imag_term = split_times(
            translator[slot_index, 0],
            translator[slot_index, 1],
            source[:, :half_size].astype(jnp.float32),
            source[:, half_size:].astype(jnp.float32),
        )
        real_sum = real_sum + present * real_term
        imag_sum = imag_sum + present * imag_term
    return jnp.concatenate([real_sum, imag_sum], axis=1)


def interpolate(pattern, theta_matrix, phi_matrix):
    box_count, part_count = (pattern.shape[0], pattern.shape[1])
    sample_grid = pattern.reshape(
        box_count * part_count, theta_matrix.shape[1], phi_matrix.shape[1]
    )
    along_phi = jnp.einsum(
        "nap,qp->naq", sample_grid, phi_matrix, preferred_element_type=jnp.float32
    ).astype(jnp.bfloat16)
    lifted = jnp.einsum("naq,ta->ntq", along_phi, theta_matrix, preferred_element_type=jnp.float32)
    return lifted.reshape(box_count, part_count, -1)


def shift_and_sum(values, slot_ids, angles):
    choose = (slot_ids[:, None] == jnp.arange(4, dtype=jnp.int32)[None, :]).astype(jnp.float32)
    cosine = jnp.dot(choose, jnp.cos(angles), precision=lax.Precision.HIGHEST)[:, None, :]
    sine_part = jnp.dot(choose, jnp.sin(angles), precision=lax.Precision.HIGHEST)[:, None, :]
    half_size = values.shape[1] // 2
    real_term, imag_term = split_times(
        cosine, sine_part, values[:, :half_size], values[:, half_size:]
    )
    shifted = jnp.concatenate([real_term, imag_term], axis=1)
    return shifted.reshape(values.shape[0] // 4, 4, values.shape[1], values.shape[2]).sum(axis=1)


def local(
    fine_out,
    fine_list,
    fine_slot,
    fine_translator,
    theta_up_fine,
    phi_up_fine,
    middle_phase,
    middle_list,
    middle_slot,
    middle_translator,
    theta_up_middle,
    phi_up_middle,
    coarse_phase,
    coarse_list,
    coarse_translator,
):
    held_boxes = fine_out.shape[0]
    dir_rank = lax.axis_index("dir")
    fine_pad = padded_2(fine_out, ((("box", "dir"), 0),), MAX_OFFSET)
    first_fine = lax.axis_index(("box", "dir")) * held_boxes
    fine_in = translate_rows(fine_pad, fine_list, first_fine, fine_translator).astype(jnp.bfloat16)
    parent_count = held_boxes // 4
    own_parent_slots = lax.dynamic_slice_in_dim(
        middle_slot, dir_rank * parent_count, parent_count, 0
    )
    lifted = interpolate(fine_out, theta_up_fine, phi_up_fine)
    child_slots = lax.dynamic_slice_in_dim(fine_slot, dir_rank * held_boxes, held_boxes, 0)
    parents = shift_and_sum(lifted, child_slots, middle_phase).astype(jnp.bfloat16)
    middle_out = lax.all_to_all(parents, "dir", split_axis=2, concat_axis=0, tiled=True)
    middle_pad = padded_2(middle_out, (("box", 0),), MAX_OFFSET)
    first_middle = lax.axis_index("box") * middle_out.shape[0]
    middle_in = translate_rows(middle_pad, middle_list, first_middle, middle_translator).astype(
        jnp.bfloat16
    )
    raised = interpolate(parents, theta_up_middle, phi_up_middle)
    coarse_own = shift_and_sum(raised, own_parent_slots, coarse_phase).astype(jnp.bfloat16)
    coarse_held = lax.all_to_all(
        lax.all_to_all(coarse_own, "box", split_axis=2, concat_axis=0, tiled=True),
        "dir",
        split_axis=2,
        concat_axis=0,
        tiled=True,
    )
    box_count = lax.axis_size("box")
    dir_count_all = lax.axis_size("dir")
    part_count = coarse_held.shape[1]
    dir_local = coarse_held.shape[2]
    ordered = coarse_held.reshape(dir_count_all, box_count, -1, part_count, dir_local)
    ordered = jnp.transpose(ordered, (1, 0, 2, 3, 4)).reshape(-1, part_count, dir_local)
    coarse_pad = jnp.pad(ordered, ((MAX_OFFSET, MAX_OFFSET), (0, 0), (0, 0)))
    coarse_in = translate_rows(coarse_pad, coarse_list, 0, coarse_translator).astype(jnp.bfloat16)
    return (fine_in, middle_in, coarse_in)


def solution(mesh):
    return jax.shard_map(
        local,
        mesh=mesh,
        in_specs=(
            P(("box", "dir"), None, None),
            P(("box", "dir"), None),
            P("box"),
            P(),
            P(),
            P(),
            P(),
            P("box", None),
            P("box"),
            P(None, None, "dir"),
            P(),
            P(),
            P(),
            P(),
            P(None, None, ("box", "dir")),
        ),
        out_specs=(
            P(("box", "dir"), None, None),
            P("box", None, "dir"),
            P(None, None, ("box", "dir")),
        ),
        check_vma=False,
    )
```

profile of v0, /device:TPU:11, one launch (start us, length us, event | category | flops | bytes accessed | tf_op | source)
XLA Modules:
  0.0 204.6 jit_solution(3008800938583719528)
XLA Ops:
  3.7 2.7 %reshape.277 = bf16[512,16,32]{2,1,0:T(8,128)(2,1)S(1)} reshape(bf16[16,32,512]{2,1,0:T(8,128)(2,1)} %param.15) | data formatting | bytes 1048576 | tf_op jit(solution)/shard_map/reshape | solution.py:61
  7.5 2.9 %convolution_bitcast_fusion.1 = f32[512,32,64]{0,1,2:T(8,128)} fusion(bf16[512,16,64]{0,2,1:T(8,128)(2,1)S(1)} %fusion.2, bf16[32,16]{0,1:T(8,128)(2,1)S(1)} %copy-done.30), kind=kOutput, calls=%fused_computation.26 | convolution fusion | flops 33554432 | bytes 5243904 | tf_op jit(solution)/shard_map/naq,ta->ntq/dot_general | solution.py:67
  10.4 9.2 %copy.48 = f32[512,32,64]{2,1,0:T(8,128)} copy(f32[512,32,64]{0,1,2:T(8,128)} %convolution_bitcast_fusion.1) | data formatting | bytes 8388608 | tf_op jit(solution)/shard_map/naq,ta->ntq/transpose | solution.py:67
  19.6 7.8 %reshape.278 = f32[16,32,2048]{2,1,0:T(8,128)} reshape(f32[512,32,64]{2,1,0:T(8,128)} %copy.48) | data formatting | bytes 8388608 | tf_op jit(solution)/shard_map/reshape | solution.py:68
  27.4 2.8 %multiply_subtract_fusion.1 = (f32[16,16,2048]{2,1,0:T(8,128)S(1)}, f32[16,16,2048]{2,1,0:T(8,128)S(1)}) fusion(f32[16,32,2048]{2,1,0:T(8,128)} %reshape.278, f32[16,2048]{1,0:T(8,128)S(1)} %fusion.248, f32[16,2048]{1,0:T(8,128)S(1)} %fusion.250), kind=kLoop, calls=%fused_computation.32 | loop fusion | flops 3145728 | bytes 8650752 | tf_op jit(solution)/shard_map/sub | solution.py:28
  31.9 2.9 %reshape.287 = bf16[4,2,32768]{2,1,0:T(2,128)(2,1)} reshape(bf16[2048,4,32]{2,1,0:T(4,128)(2,1)S(1)} %bitcast.128) | data formatting | bytes 1048576
  34.9 4.9 %all-to-all-start = ((bf16[4,2,32768]{2,1,0:T(2,128)(2,1)}), bf16[4,2,32768]{2,1,0:T(2,128)(2,1)}, u32[]{:S(2)}, u32[]{:S(2)}) async-start(bf16[4,2,32768]{2,1,0:T(2,128)(2,1)} %reshape.287), calls=%async_computation | async-start | bytes 1048576 | tf_op jit(solution)/shard_map/all_to_all | solution.py:112
  40.5 3.5 %collective-permute-start = (bf16[7,32,512]{2,1,0:T(8,128)(2,1)}, bf16[7,32,512]{2,1,0:T(8,128)(2,1)}, u32[]{:S(2)}, u32[]{:S(2)}) collective-permute-start(bf16[7,32,512]{2,1,0:T(8,128)(2,1)} %get-tuple-element.47), channel_id=1, source_target_pairs={{0,1},{1,2},{2,3},{3,4},{4,5},{5,6},{6,7},{7,8},{8,9},{9,10},{10,1... | collective-permute-start | bytes 688136 | tf_op jit(solution)/shard_map/ppermute | solution.py:17
  44.1 1.9 collective-permute-start.1
  51.0 3.0 %convolution_bitcast_fusion = f32[128,64,128]{2,1,0:T(8,128)} fusion(bf16[128,32,64]{2,1,0:T(8,128)(2,1)S(1)} %convert_element_type.577, bf16[128,64]{0,1:T(8,128)(2,1)S(1)} %copy-done, bf16[64,32]{0,1:T(8,128)(2,1)S(1)} %copy-done.26), kind=kOutput, calls=%fused_computation.25 | convolution fusion | flops 134742016 | bytes 4739072 | tf_op jit(solution)/shard_map/naq,ta->ntq/dot_general | solution.py:67
  54.0 5.0 %reshape.280 = f32[4,32,8192]{2,1,0:T(8,128)} reshape(f32[128,64,128]{2,1,0:T(8,128)} %convolution_bitcast_fusion) | data formatting | bytes 8388608 | tf_op jit(solution)/shard_map/reshape | solution.py:68
  59.0 2.8 %multiply_subtract_fusion = (f32[4,16,8192]{2,1,0:T(8,128)S(1)}, f32[4,16,8192]{2,1,0:T(8,128)S(1)}) fusion(f32[4,32,8192]{2,1,0:T(8,128)} %reshape.280, f32[4,8192]{1,0:T(4,128)S(1)} %fusion.244, f32[4,8192]{1,0:T(4,128)S(1)} %fusion.246), kind=kLoop, calls=%fused_computation.30 | loop fusion | flops 3145728 | bytes 8650752 | tf_op jit(solution)/shard_map/sub | solution.py:28
  62.9 6.7 %copy.52 = bf16[1,32,8192]{1,0,2:T(2,128)(2,1)} copy(bf16[1,32,8192]{2,1,0:T(8,128)(2,1)S(1)} %bitcast.134) | data formatting | bytes 1048576 | tf_op jit(solution)/shard_map/convert_element_type | solution.py:119
  70.1 45.2 %reduce.2 = bf16[8192,32]{1,0:T(8,128)(2,1)S(1)} reduce(bf16[8192,1,32]{2,1,0:T(2,128)(2,1)} %bitcast.123, bf16[]{:T(256)} %broadcast.298), dimensions={1}, to_apply=%bitcast.117.reduce_sub_computation | reduce | bytes 1048578
  115.4 2.7 %reshape.289 = bf16[8,2,16384]{2,1,0:T(2,128)(2,1)} reshape(bf16[8192,32]{1,0:T(8,128)(2,1)S(1)} %reduce.2) | data formatting | bytes 1048576
  131.4 1.7 fusion.221
  133.2 5.7 %all-to-all-start.1 = ((bf16[8,2,16384]{2,1,0:T(2,128)(2,1)}), bf16[8,2,16384]{2,1,0:T(2,128)(2,1)S(1)}, u32[]{:S(2)}, u32[]{:S(2)}) async-start(bf16[8,2,16384]{2,1,0:T(2,128)(2,1)} %reshape.289), calls=%async_computation.1 | async-start | bytes 1048576 | tf_op jit(solution)/shard_map/all_to_all | solution.py:121
  138.9 4.1 %reshape.288 = bf16[2048,4,32]{2,1,0:T(4,128)(2,1)} reshape(bf16[4,2,32768]{2,1,0:T(2,128)(2,1)} %all-to-all-done) | data formatting | bytes 1048576
  143.0 2.9 %copy.51 = bf16[4,4,32,512]{3,2,1,0:T(8,128)(2,1)S(1)} copy(bf16[4,4,32,512]{2,1,3,0:T(4,128)(2,1)} %bitcast.125) | data formatting | bytes 1048576 | tf_op jit(solution)/shard_map/all_to_all | solution.py:112
  146.0 3.1 %collective-permute-start.2 = (bf16[7,32,512]{2,1,0:T(8,128)(2,1)S(1)}, bf16[7,32,512]{2,1,0:T(8,128)(2,1)S(1)}, u32[]{:S(2)}, u32[]{:S(2)}) collective-permute-start(bf16[7,32,512]{2,1,0:T(8,128)(2,1)S(1)} %get-tuple-element.44), channel_id=1, source_target_pairs={{0,4},{4,8},{8,12},{12,16},{16,20},{20,24},{24,28},{1,5},{5,9},{9,... | collective-permute-start | bytes 688136 | tf_op jit(solution)/shard_map/ppermute | solution.py:17
  149.1 2.2 %collective-permute-start.3 = (bf16[7,32,512]{2,1,0:T(8,128)(2,1)S(1)}, bf16[7,32,512]{2,1,0:T(8,128)(2,1)S(1)}, u32[]{:S(2)}, u32[]{:S(2)}) collective-permute-start(bf16[7,32,512]{2,1,0:T(8,128)(2,1)S(1)} %get-tuple-element.43), channel_id=1, source_target_pairs={{4,0},{8,4},{12,8},{16,12},{20,16},{24,20},{28,24},{5,1},{9,5},{13... | collective-permute-start | bytes 688136 | tf_op jit(solution)/shard_map/ppermute | solution.py:19
  151.5 1.9 fusion.220
  155.0 5.0 %collective-permute-done.3 = bf16[7,32,512]{2,1,0:T(8,128)(2,1)S(1)} collective-permute-done((bf16[7,32,512]{2,1,0:T(8,128)(2,1)S(1)}, bf16[7,32,512]{2,1,0:T(8,128)(2,1)S(1)}, u32[]{:S(2)}, u32[]{:S(2)}) %collective-permute-start.3) | collective-permute-done | bytes 229408 | tf_op jit(solution)/shard_map/ppermute | solution.py:19
  160.7 5.4 %fusion.219 = bf16[16,16,512]{2,1,0:T(8,128)(2,1)S(1)} fusion(f32[512]{0:T(512)S(1)} %bitcast.182, f32[512]{0:T(512)S(1)} %bitcast.184, f32[16]{0:T(128)S(1)} %copy-done.46, f32[512]{0:T(512)S(1)} %bitcast.140, f32[512]{0:T(512)S(1)} %bitcast.142, f32[16]{0:T(128)S(1)} %copy-done.45, f32[512]{0:T(512)S(1)} %bitcast.144, f32[512]{0:T(512)S(1)} %bitcast.146, ...), kind=kLoop, calls=%fused_computation.444 | loop fusion | flops 20447232 | bytes 1295104 | tf_op jit(solution)/shard_map/convert.2
  166.1 4.5 %reshape.290 = bf16[8192,1,32]{2,1,0:T(2,128)(2,1)} reshape(bf16[8,2,16384]{2,1,0:T(2,128)(2,1)S(1)} %all-to-all-done.1) | data formatting | bytes 1048576
  170.6 8.0 %copy.53 = bf16[1,32,8192]{2,1,0:T(8,128)(2,1)S(1)} copy(bf16[1,32,8192]{1,0,2:T(2,128)(2,1)} %bitcast.124) | data formatting | bytes 1048576 | tf_op jit(solution)/shard_map/all_to_all | solution.py:121
  179.0 1.8 copy.54
  180.8 2.9 %reshape.291 = bf16[4,2,32768]{2,1,0:T(2,128)(2,1)} reshape(bf16[1024,8,32]{2,1,0:T(8,128)(2,1)S(1)} %bitcast.126) | data formatting | bytes 1048576
  183.7 4.3 %all-to-all-start.2 = ((bf16[4,2,32768]{2,1,0:T(2,128)(2,1)}), bf16[4,2,32768]{2,1,0:T(2,128)(2,1)S(1)}, u32[]{:S(2)}, u32[]{:S(2)}) async-start(bf16[4,2,32768]{2,1,0:T(2,128)(2,1)} %reshape.291), calls=%async_computation.2 | async-start | bytes 1048576 | tf_op jit(solution)/shard_map/all_to_all | solution.py:120
  188.0 6.1 %fusion.218 = bf16[16,16,512]{2,1,0:T(8,128)(2,1)S(1)} fusion(f32[512]{0:T(512)S(1)} %bitcast.183, f32[512]{0:T(512)S(1)} %bitcast.185, f32[16]{0:T(128)} %convert_element_type.573, f32[512]{0:T(512)S(1)} %bitcast.141, f32[512]{0:T(512)S(1)} %bitcast.143, f32[16]{0:T(128)} %convert_element_type.570, f32[512]{0:T(512)S(1)} %bitcast.145, ...), kind=kLoop, calls=%fused_computation.443 | loop fusion | flops 20447232 | bytes 1295104 | tf_op jit(solution)/shard_map/convert.3
  199.4 2.2 %fusion.217 = bf16[32,16,256]{2,1,0:T(8,128)(2,1)S(1)} fusion(f32[256]{0:T(256)S(1)} %bitcast.278, f32[256]{0:T(256)S(1)} %bitcast.280, f32[32]{0:T(128)S(1)} %copy-done.58, f32[256]{0:T(256)S(1)} %bitcast.236, f32[256]{0:T(256)S(1)} %bitcast.238, f32[32]{0:T(128)S(1)} %copy-done.57, f32[256]{0:T(256)S(1)} %bitcast.240, f32[256]{0:T(256)S(1)} %bitcast.242, ...), kind=kLoop, calls=%fused_computation.442 | loop fusion | flops 11010048 | bytes 812544 | tf_op jit(solution)/shard_map/convert
  201.6 2.2 %fusion.216 = bf16[32,16,256]{2,1,0:T(8,128)(2,1)S(1)} fusion(f32[256]{0:T(256)S(1)} %bitcast.279, f32[256]{0:T(256)S(1)} %bitcast.281, f32[32]{0:T(128)S(1)} %copy-done.58, f32[256]{0:T(256)S(1)} %bitcast.237, f32[256]{0:T(256)S(1)} %bitcast.239, f32[32]{0:T(128)S(1)} %copy-done.57, f32[256]{0:T(256)S(1)} %bitcast.241, f32[256]{0:T(256)S(1)} %bitcast.243, ...), kind=kLoop, calls=%fused_computation.441 | loop fusion | flops 11010048 | bytes 812544 | tf_op jit(solution)/shard_map/convert.1
  (262 shorter events, 34.5 us)
Async XLA Ops:
  0.6 50.3 %copy-start = (bf16[128,64]{0,1:T(8,128)(2,1)S(1)}, bf16[128,64]{0,1:T(8,128)(2,1)}, u32[]{:S(2)}) copy-start(bf16[128,64]{0,1:T(8,128)(2,1)} %param.26) | copy-start | bytes 49156
  34.9 12.2 %copy-start.83 = (s32[16]{0:T(128)S(1)}, s32[16]{0:T(128)}, u32[]{:S(2)}) copy-start(s32[16]{0:T(128)} %param.23) | copy-start | bytes 196
  34.9 12.3 %copy-start.5 = (f32[4,8192]{1,0:T(4,128)S(1)}, f32[4,8192]{1,0:T(4,128)}, u32[]{:S(2)}) copy-start(f32[4,8192]{1,0:T(4,128)} %param.27) | copy-start | bytes 393220
  34.9 14.6 %copy-start.8 = (f32[12,2,256]{2,1,0:T(2,128)S(1)}, f32[12,2,256]{2,1,0:T(2,128)}, u32[]{:S(2)}) copy-start(f32[12,2,256]{2,1,0:T(2,128)} %param.29) | copy-start | bytes 73732
  34.9 15.9 %copy-start.6 = (f32[12,2,512]{2,1,0:T(2,128)S(1)}, f32[12,2,512]{2,1,0:T(2,128)}, u32[]{:S(2)}) copy-start(f32[12,2,512]{2,1,0:T(2,128)} %param.24) | copy-start | bytes 147460
  34.9 16.1 %copy-start.26 = (bf16[64,32]{0,1:T(8,128)(2,1)S(1)}, bf16[64,32]{0,1:T(8,128)(2,1)}, u32[]{:S(2)}) copy-start(bf16[64,32]{0,1:T(8,128)(2,1)} %param.25) | copy-start | bytes 12292
  34.9 98.3 %all-to-all-start = ((bf16[4,2,32768]{2,1,0:T(2,128)(2,1)}), bf16[4,2,32768]{2,1,0:T(2,128)(2,1)}, u32[]{:S(2)}, u32[]{:S(2)}) async-start(bf16[4,2,32768]{2,1,0:T(2,128)(2,1)} %reshape.287), calls=%async_computation | async-start | bytes 1048576 | tf_op jit(solution)/shard_map/all_to_all | solution.py:112
  40.5 88.8 %collective-permute-start = (bf16[7,32,512]{2,1,0:T(8,128)(2,1)}, bf16[7,32,512]{2,1,0:T(8,128)(2,1)}, u32[]{:S(2)}, u32[]{:S(2)}) collective-permute-start(bf16[7,32,512]{2,1,0:T(8,128)(2,1)} %get-tuple-element.47), channel_id=1, source_target_pairs={{0,1},{1,2},{2,3},{3,4},{4,5},{5,6},{6,7},{7,8},{8,9},{9,10},{10,1... | collective-permute-start | bytes 688136 | tf_op jit(solution)/shard_map/ppermute | solution.py:17
  44.1 86.3 %collective-permute-start.1 = (bf16[7,32,512]{2,1,0:T(8,128)(2,1)S(1)}, bf16[7,32,512]{2,1,0:T(8,128)(2,1)}, u32[]{:S(2)}, u32[]{:S(2)}) collective-permute-start(bf16[7,32,512]{2,1,0:T(8,128)(2,1)S(1)} %get-tuple-element.48), channel_id=1, source_target_pairs={{1,0},{2,1},{3,2},{4,3},{5,4},{6,5},{7,6},{8,7},{9,8},{10,9},{11,1... | collective-permute-start | bytes 688136 | tf_op jit(solution)/shard_map/ppermute | solution.py:19
  124.7 35.3 %copy-start.31 = (f32[16]{0:T(128)}, f32[16]{0:T(128)S(1)}, u32[]{:S(2)}) copy-start(f32[16]{0:T(128)S(1)} %convert_element_type.538) | copy-start | bytes 196
  124.7 35.3 %copy-start.33 = (f32[16]{0:T(128)}, f32[16]{0:T(128)S(1)}, u32[]{:S(2)}) copy-start(f32[16]{0:T(128)S(1)} %convert_element_type.543) | copy-start | bytes 196
  124.7 35.3 %copy-start.35 = (f32[16]{0:T(128)}, f32[16]{0:T(128)S(1)}, u32[]{:S(2)}) copy-start(f32[16]{0:T(128)S(1)} %convert_element_type.546) | copy-start | bytes 196
  124.7 35.3 %copy-start.37 = (f32[16]{0:T(128)}, f32[16]{0:T(128)S(1)}, u32[]{:S(2)}) copy-start(f32[16]{0:T(128)S(1)} %convert_element_type.549) | copy-start | bytes 196
  133.2 32.9 %all-to-all-start.1 = ((bf16[8,2,16384]{2,1,0:T(2,128)(2,1)}), bf16[8,2,16384]{2,1,0:T(2,128)(2,1)S(1)}, u32[]{:S(2)}, u32[]{:S(2)}) async-start(bf16[8,2,16384]{2,1,0:T(2,128)(2,1)} %reshape.289), calls=%async_computation.1 | async-start | bytes 1048576 | tf_op jit(solution)/shard_map/all_to_all | solution.py:121
  143.0 8.4 %copy-start.68 = (f32[16]{0:T(128)S(1)}, f32[16]{0:T(128)}, u32[]{:S(2)}) copy-start(f32[16]{0:T(128)} %copy-done.67) | copy-start | bytes 196
  143.0 8.4 %copy-start.70 = (f32[16]{0:T(128)S(1)}, f32[16]{0:T(128)}, u32[]{:S(2)}) copy-start(f32[16]{0:T(128)} %copy-done.69) | copy-start | bytes 196
  143.0 8.4 %copy-start.72 = (f32[16]{0:T(128)S(1)}, f32[16]{0:T(128)}, u32[]{:S(2)}) copy-start(f32[16]{0:T(128)} %copy-done.71) | copy-start | bytes 196
  143.0 8.4 %copy-start.74 = (f32[16]{0:T(128)S(1)}, f32[16]{0:T(128)}, u32[]{:S(2)}) copy-start(f32[16]{0:T(128)} %copy-done.73) | copy-start | bytes 196
  143.0 8.4 %copy-start.76 = (f32[16]{0:T(128)S(1)}, f32[16]{0:T(128)}, u32[]{:S(2)}) copy-start(f32[16]{0:T(128)} %copy-done.75) | copy-start | bytes 196
  143.0 8.4 %copy-start.78 = (f32[16]{0:T(128)S(1)}, f32[16]{0:T(128)}, u32[]{:S(2)}) copy-start(f32[16]{0:T(128)} %copy-done.77) | copy-start | bytes 196
  146.0 9.0 %collective-permute-start.2 = (bf16[7,32,512]{2,1,0:T(8,128)(2,1)S(1)}, bf16[7,32,512]{2,1,0:T(8,128)(2,1)S(1)}, u32[]{:S(2)}, u32[]{:S(2)}) collective-permute-start(bf16[7,32,512]{2,1,0:T(8,128)(2,1)S(1)} %get-tuple-element.44), channel_id=1, source_target_pairs={{0,4},{4,8},{8,12},{12,16},{16,20},{20,24},{24,28},{1,5},{5,9},{9,... | collective-permute-start | bytes 688136 | tf_op jit(solution)/shard_map/ppermute | solution.py:17
  149.1 11.6 %copy-start.39 = (f32[16]{0:T(128)S(1)}, f32[16]{0:T(128)}, u32[]{:S(2)}) copy-start(f32[16]{0:T(128)} %convert_element_type.552) | copy-start | bytes 196
  149.1 11.6 %copy-start.40 = (f32[16]{0:T(128)S(1)}, f32[16]{0:T(128)}, u32[]{:S(2)}) copy-start(f32[16]{0:T(128)} %convert_element_type.555) | copy-start | bytes 196
  149.1 11.6 %copy-start.41 = (f32[16]{0:T(128)S(1)}, f32[16]{0:T(128)}, u32[]{:S(2)}) copy-start(f32[16]{0:T(128)} %convert_element_type.558) | copy-start | bytes 196
  149.1 11.6 %copy-start.42 = (f32[16]{0:T(128)S(1)}, f32[16]{0:T(128)}, u32[]{:S(2)}) copy-start(f32[16]{0:T(128)} %convert_element_type.561) | copy-start | bytes 196
  149.1 11.6 %copy-start.43 = (f32[16]{0:T(128)S(1)}, f32[16]{0:T(128)}, u32[]{:S(2)}) copy-start(f32[16]{0:T(128)} %convert_element_type.564) | copy-start | bytes 196
  149.1 11.6 %copy-start.44 = (f32[16]{0:T(128)S(1)}, f32[16]{0:T(128)}, u32[]{:S(2)}) copy-start(f32[16]{0:T(128)} %convert_element_type.567) | copy-start | bytes 196
  149.1 11.6 %copy-start.45 = (f32[16]{0:T(128)S(1)}, f32[16]{0:T(128)}, u32[]{:S(2)}) copy-start(f32[16]{0:T(128)} %convert_element_type.570) | copy-start | bytes 196
  149.1 11.6 %copy-start.46 = (f32[16]{0:T(128)S(1)}, f32[16]{0:T(128)}, u32[]{:S(2)}) copy-start(f32[16]{0:T(128)} %convert_element_type.573) | copy-start | bytes 196
  149.1 10.8 %collective-permute-start.3 = (bf16[7,32,512]{2,1,0:T(8,128)(2,1)S(1)}, bf16[7,32,512]{2,1,0:T(8,128)(2,1)S(1)}, u32[]{:S(2)}, u32[]{:S(2)}) collective-permute-start(bf16[7,32,512]{2,1,0:T(8,128)(2,1)S(1)} %get-tuple-element.43), channel_id=1, source_target_pairs={{4,0},{8,4},{12,8},{16,12},{20,16},{24,20},{28,24},{5,1},{9,5},{13... | collective-permute-start | bytes 688136 | tf_op jit(solution)/shard_map/ppermute | solution.py:19
  155.0 15.7 %copy-start.3 = (bf16[7,32,512]{2,1,0:T(8,128)(2,1)}, bf16[7,32,512]{2,1,0:T(8,128)(2,1)S(1)}, u32[]{:S(2)}) copy-start(bf16[7,32,512]{2,1,0:T(8,128)(2,1)S(1)} %collective-permute-done.2) | copy-start | bytes 688132
  183.7 12.3 %all-to-all-start.2 = ((bf16[4,2,32768]{2,1,0:T(2,128)(2,1)}), bf16[4,2,32768]{2,1,0:T(2,128)(2,1)S(1)}, u32[]{:S(2)}, u32[]{:S(2)}) async-start(bf16[4,2,32768]{2,1,0:T(2,128)(2,1)} %reshape.291), calls=%async_computation.2 | async-start | bytes 1048576 | tf_op jit(solution)/shard_map/all_to_all | solution.py:120
  (59 other events, 220.0 us)
where the time goes:
time: 208 us; the launch traced here: 205 us
  other arithmetic  85.1 us (41%)
  local copies, waits for them, and re-layouts  73.2 us (35%)
  starting transfers between devices  25.6 us (12%)
  matrix products  11.5 us (6%)
  waiting for transfers between devices  6.88 us (3%)
  between operations  2.3 us (1%)
    unnamed x1, other arithmetic  45.2 us
    unnamed x177, local copies, waits for them, and re-layouts  21 us
    another operation x6, other arithmetic  19.3 us
    reshape x2, local copies, waits for them, and re-layouts, interpolate(): return lifted.reshape(box_count, part_count, -1)  12.8 us
    convert_element_type x36, other arithmetic, translate_rows(): jnp.any(entries == (box_ids + offset)[:, None], axis=1).astype(jnp.float32)  11 us
    all_to_all x3, local copies, waits for them, and re-layouts, local(): lax.all_to_all(coarse_own, 'box', split_axis=2, concat_axis=0, tiled=True)  9.79 us
    transpose x1, local copies, waits for them, and re-layouts, interpolate(): jnp.einsum('naq,ta->ntq', along_phi, theta_matrix, preferred_element_type...  9.17 us
    convert_element_type x1, local copies, waits for them, and re-layouts, local(): shift_and_sum(raised, own_parent_slots, coarse_phase).astype(jnp.bfloat16)  6.73 us
  transfers between devices with their start and end apart: 7, of which 3 were waited for; matrix products, arithmetic and copies ran while one was open for 53% of the time, Pallas kernels for 0%

commit v1 on v0

v1 whole, which is shorter than its diff:
```python
import functools

import jax
import jax.numpy as jnp
from jax import lax
from jax.experimental import pallas as pl
from jax.experimental.pallas import tpu as pltpu
from jax.sharding import PartitionSpec as P

MAX_OFFSET = 7
LANES = 128
F32 = jnp.float32
BF16 = jnp.bfloat16
MESH = pl.DeviceIdType.MESH


def offsets_used():
    return list(range(-MAX_OFFSET, -1)) + list(range(2, MAX_OFFSET + 1))


def presence(entries, first_box):
    ids = first_box + jnp.arange(entries.shape[0], dtype=jnp.int32)
    wanted = ids[:, None] + jnp.array(offsets_used(), jnp.int32)[None, :]
    return jnp.any(entries[:, None, :] == wanted[:, :, None], axis=2).astype(F32)


def iota(shape, dim):
    return lax.broadcasted_iota(jnp.int32, shape, dim)


def one_hot(cond):
    return jnp.where(cond, 1.0, 0.0).astype(BF16)


def dot(a, b, dims=((1,), (0,))):
    return lax.dot_general(a, b, (dims, ((), ())), preferred_element_type=F32)


def kron_identity(matrix, width):
    rows, cols = matrix.shape
    shift = width.bit_length() - 1
    left = one_hot((iota((rows * width, rows), 0) >> shift) == iota((rows * width, rows), 1))
    right = one_hot(iota((cols, cols * width), 0) == (iota((cols, cols * width), 1) >> shift))
    full = dot(dot(left, matrix).astype(BF16), right)
    shape = (rows * width, cols * width)
    keep = (iota(shape, 0) & (width - 1)) == (iota(shape, 1) & (width - 1))
    return jnp.where(keep, full, 0.0).astype(BF16)


def phi_blocks(phi, pair):
    q, p = phi.shape
    thetas = 256 // (pair * p)
    rows, cols = pair * thetas * p, thetas * pair * q
    left = one_hot((iota((rows, p), 0) & (p - 1)) == iota((rows, p), 1))
    right = one_hot(iota((q, cols), 0) == (iota((q, cols), 1) & (q - 1)))
    full = dot(dot(left, phi, ((1,), (1,))).astype(BF16), right)
    shape = (rows, cols)
    r, c = iota(shape, 0), iota(shape, 1)
    ps, qs = p.bit_length() - 1, q.bit_length() - 1
    ths, prs = thetas.bit_length() - 1, pair.bit_length() - 1
    row_t, row_h = (r >> ps) & (thetas - 1), r >> (ps + ths)
    col_h, col_t = (c >> qs) & (pair - 1), c >> (qs + prs)
    return jnp.where((row_t == col_t) & (row_h == col_h), full, 0.0).astype(BF16)


def translate(groups, tiles, load, mask_ref, factor, store):
    def step(it, _):
        g, lt = lax.div(it, tiles), lax.rem(it, tiles)
        sources = [load(g, j, lt).astype(F32) for j in range(12)]
        half = sources[0].shape[0] // 2
        for i in range(4):
            real, imag = None, None
            for s, offset in enumerate(offsets_used()):
                j = 4 + i + offset
                if j < 0 or j > 11:
                    continue
                m = mask_ref[4 * g + i, s]
                a, b = factor(s, 0, lt) * m, factor(s, 1, lt) * m
                pr, pi = sources[j][:half], sources[j][half:]
                tr, ti = a * pr - b * pi, a * pi + b * pr
                real = tr if real is None else real + tr
                imag = ti if imag is None else imag + ti
            store(4 * g + i, lt, real.astype(BF16), imag.astype(BF16))
        return 0

    lax.fori_loop(0, groups * tiles, step, 0)


def lane_tile(lt):
    return pl.ds(pl.multiple_of(lt * LANES, LANES), LANES)


def kernel(
    nb, nd,
    fine_hbm, fine_mask, fine_slot, fine_tr, theta_f, phi_f, mid_phase,
    mid_mask, mid_slot, mid_tr, theta_m, phi_m, coarse_phase, coarse_mask, coarse_tr,
    fine_in, mid_in, coarse_in,
    fpad, par, mrecv, crs, crecv, along1, lift1, along2, lift2,
    cosm, sinm, cosc, sinc,
    load_sem, fsend, frecv, msend, mrecv_sem, csend, crecv_sem,
):
    n = nb * nd
    b, d = lax.axis_index("box"), lax.axis_index("dir")
    me = b * nd + d
    held = fine_in.shape[0]
    t_mid, t_coarse = theta_f.shape[0], theta_m.shape[0]
    mid_tiles = par.shape[0]
    mlt = mid_tiles // nd
    ctiles = crecv.shape[1]
    ntile = t_coarse // ctiles
    share = n // ntile

    def device(i):
        return (lax.div(i, nd), lax.rem(i, nd))

    fine_load = pltpu.make_async_copy(fine_hbm, fpad.at[pl.ds(4, held)], load_sem)
    fine_load.start()
    barrier = pltpu.get_barrier_semaphore()

    def greet(j, _):
        pl.semaphore_signal(
            barrier, inc=1, device_id=device(lax.rem(me + 1 + j, n)), device_id_type=MESH
        )
        return 0

    lax.fori_loop(0, n - 1, greet, 0)

    bd1 = phi_blocks(phi_f[...], 2)
    k1 = kron_identity(theta_f[...], 16)
    bd2 = phi_blocks(phi_m[...], 1)
    k2 = kron_identity(theta_m[...], 8)
    cosc[...] = jnp.cos(coarse_phase[...])
    sinc[...] = jnp.sin(coarse_phase[...])
    cosine, sine = jnp.cos(mid_phase[...]), jnp.sin(mid_phase[...])
    low = iota((t_mid, LANES), 1) < LANES // 2
    for u in range(2):
        for k in range(4):
            s0 = fine_slot[d * held + 8 * u + k]
            s1 = fine_slot[d * held + 8 * u + 4 + k]
            for table, values in ((cosm, cosine), (sinm, sine)):
                first = values[3]
                second = values[3]
                for s in range(3):
                    first = jnp.where(s0 == s, values[s], first)
                    second = jnp.where(s1 == s, values[s], second)
                table[4 * u + k] = jnp.where(low, first, second)

    zeros4 = jnp.zeros((4,) + fpad.shape[1:], BF16)

    @pl.when(me == 0)
    def _():
        fpad[0:4] = zeros4

    @pl.when(me == n - 1)
    def _():
        fpad[4 + held:8 + held] = zeros4

    @pl.when(b == 0)
    def _():
        mrecv[0] = jnp.zeros(mrecv.shape[1:], BF16)

    @pl.when(b == nb - 1)
    def _():
        mrecv[nd + 1] = jnp.zeros(mrecv.shape[1:], BF16)

    crecv[0:4] = jnp.zeros((4,) + crecv.shape[1:], BF16)
    crecv[n + 4:n + 8] = jnp.zeros((4,) + crecv.shape[1:], BF16)

    fine_load.wait()

    for g in range(4):
        part = fpad[4:4 + held, :, g * LANES:(g + 1) * LANES]
        part = part.reshape(held // 8, 2, 4 * 32, LANES)
        pair = jnp.concatenate([part[:, 0], part[:, 1]], axis=-1).reshape(-1, 2 * LANES)
        out = dot(pair, bd1).astype(BF16)
        for i in range(4):
            along1[4 * g + i] = out[:, i * LANES:(i + 1) * LANES]
    for uk in range(8):
        rhs = jnp.concatenate(
            [
                along1[:, uk * 32:uk * 32 + 16, :].reshape(256, LANES),
                along1[:, uk * 32 + 16:uk * 32 + 32, :].reshape(256, LANES),
            ],
            axis=-1,
        )
        lift1[uk] = dot(k1, rhs).reshape(t_mid, 16, 2 * LANES)

    lower = iota((16, LANES), 1) < LANES // 2

    def parents_step(v, _):
        for u in range(2):
            sums = []
            for e in range(2):
                t2 = 2 * v + e
                real, imag = None, None
                for k in range(4):
                    uk = 4 * u + k
                    value = lift1[uk, t2]
                    vr, vi = value[:, :LANES], value[:, LANES:]
                    co = cosm[uk, pl.ds(t2, 1), :]
                    si = sinm[uk, pl.ds(t2, 1), :]
                    tr, ti = co * vr - si * vi, co * vi + si * vr
                    real = tr if real is None else real + tr
                    imag = ti if imag is None else imag + ti
                sums.append((real, imag))
            for c in range(2):
                s0, s1 = sums[0][c], sums[1][c]
                par[v, 2 * u, 16 * c:16 * c + 16, :] = jnp.where(
                    lower, s0, pltpu.roll(s1, LANES // 2, 1)
                ).astype(BF16)
                par[v, 2 * u + 1, 16 * c:16 * c + 16, :] = jnp.where(
                    lower, pltpu.roll(s0, LANES // 2, 1), s1
                ).astype(BF16)
        return 0

    lax.fori_loop(0, mid_tiles, parents_step, 0)

    pl.semaphore_wait(barrier, n - 1)

    def fine_copy(to_next):
        peer = me + 1 if to_next else me - 1
        return pltpu.make_async_remote_copy(
            src_ref=fpad.at[pl.ds(held, 4)] if to_next else fpad.at[pl.ds(4, 4)],
            dst_ref=fpad.at[pl.ds(0, 4)] if to_next else fpad.at[pl.ds(4 + held, 4)],
            send_sem=fsend.at[0 if to_next else 1],
            recv_sem=frecv.at[0 if to_next else 1],
            device_id=device(peer),
            device_id_type=MESH,
        )

    def mid_copy(dd, box, slot, sem):
        return pltpu.make_async_remote_copy(
            src_ref=par.at[pl.ds(dd * mlt, mlt)],
            dst_ref=mrecv.at[slot],
            send_sem=msend.at[sem],
            recv_sem=mrecv_sem.at[slot],
            device_id=(box, dd),
            device_id_type=MESH,
        )

    def coarse_copy(tile, dest):
        return pltpu.make_async_remote_copy(
            src_ref=crs.at[pl.ds(tile * ctiles, ctiles)],
            dst_ref=crecv.at[4 + me],
            send_sem=csend.at[dest],
            recv_sem=crecv_sem.at[me],
            device_id=device(dest),
            device_id_type=MESH,
        )

    def each_mid(act):
        def own(j, _):
            dd = lax.rem(d + 1 + j, nd)
            act(mid_copy(dd, b, 1 + d, dd))
            return 0

        lax.fori_loop(0, nd - 1, own, 0)

        @pl.when((d == nd - 1) & (b < nb - 1))
        def _():
            def up(dd, _):
                act(mid_copy(dd, b + 1, 0, nd + dd))
                return 0

            lax.fori_loop(0, nd, up, 0)

        @pl.when((d == 0) & (b > 0))
        def _():
            def down(dd, _):
                act(mid_copy(dd, b - 1, nd + 1, nd + dd))
                return 0

            lax.fori_loop(0, nd, down, 0)

    each_mid(lambda c: c.start())
    mrecv[1 + d] = par[pl.ds(d * mlt, mlt)]

    @pl.when(me < n - 1)
    def _():
        fine_copy(True).start()

    @pl.when(me > 0)
    def _():
        fine_copy(False).start()

    rows = par.shape[1] * par.shape[2]
    for g in range(mid_tiles // 2):
        lhs = jnp.concatenate(
            [par[2 * g].reshape(rows, LANES), par[2 * g + 1].reshape(rows, LANES)], axis=-1
        )
        out = dot(lhs, bd2)
        for i in range(4):
            along2[4 * g + i] = out[:, i * LANES:(i + 1) * LANES]
    for k in range(4):
        for cg in range(2):
            r0 = k * 32 + cg * 8
            rhs = jnp.concatenate(
                [
                    along2[:, r0:r0 + 8, :].reshape(256, LANES),
                    along2[:, r0 + 16:r0 + 24, :].reshape(256, LANES),
                ],
                axis=-1,
            ).astype(BF16)
            lift2[2 * k + cg] = dot(k2, rhs).reshape(t_coarse, 8, 2 * LANES)

    slots = [mid_slot[d * 4 + k] for k in range(4)]
    my_tile = lax.div(me, share)

    def coarse_step(j, _):
        tile = lax.rem(my_tile + 1 + j, ntile)
        for i in range(ctiles):
            t2 = tile * ctiles + i
            reals, imags = [None, None], [None, None]
            for k in range(4):
                co = cosc[slots[k], pl.ds(t2, 1), :]
                si = sinc[slots[k], pl.ds(t2, 1), :]
                for cg in range(2):
                    value = lift2[2 * k + cg, t2]
                    vr, vi = value[:, :LANES], value[:, LANES:]
                    tr, ti = co * vr - si * vi, co * vi + si * vr
                    reals[cg] = tr if k == 0 else reals[cg] + tr
                    imags[cg] = ti if k == 0 else imags[cg] + ti
            crs[t2, 0:16, :] = jnp.concatenate(reals, axis=0).astype(BF16)
            crs[t2, 16:32, :] = jnp.concatenate(imags, axis=0).astype(BF16)
        for r in range(share):
            dest = tile * share + r

            @pl.when(dest != me)
            def _():
                coarse_copy(tile, dest).start()

        return 0

    lax.fori_loop(0, ntile, coarse_step, 0)
    crecv[4 + me] = crs[pl.ds(my_tile * ctiles, ctiles)]

    @pl.when(me > 0)
    def _():
        fine_copy(True).wait_recv()

    @pl.when(me < n - 1)
    def _():
        fine_copy(False).wait_recv()

    def fine_store(i, lt, real, imag):
        fine_in[i, 0:16, lane_tile(lt)] = real
        fine_in[i, 16:32, lane_tile(lt)] = imag

    translate(
        held // 4,
        fine_in.shape[2] // LANES,
        lambda g, j, lt: fpad[4 * g + j, :, lane_tile(lt)],
        fine_mask,
        lambda s, c, lt: fine_tr[s, c:c + 1, lane_tile(lt)],
        fine_store,
    )

    def mid_wait(slot):
        mid_copy(0, b, slot, 0).wait_recv()

    def own_wait(j, _):
        mid_wait(1 + lax.rem(d + 1 + j, nd))
        return 0

    lax.fori_loop(0, nd - 1, own_wait, 0)

    @pl.when(b > 0)
    def _():
        mid_wait(0)

    @pl.when(b < nb - 1)
    def _():
        mid_wait(nd + 1)

    def mid_store(i, lt, real, imag):
        mid_in[i, 0:16, lane_tile(lt)] = real
        mid_in[i, 16:32, lane_tile(lt)] = imag

    translate(
        nd,
        mlt,
        lambda g, j, lt: mrecv[g + j // 4, lt, j % 4],
        mid_mask,
        lambda s, c, lt: mid_tr[s, c:c + 1, lane_tile(lt)],
        mid_store,
    )

    def coarse_wait(j, _):
        source = lax.rem(me + n - 1 - j, n)
        pltpu.make_async_remote_copy(
            src_ref=crs.at[pl.ds(0, ctiles)],
            dst_ref=crecv.at[4 + source],
            send_sem=csend.at[source],
            recv_sem=crecv_sem.at[source],
            device_id=device(source),
            device_id_type=MESH,
        ).wait_recv()
        return 0

    lax.fori_loop(0, n - 1, coarse_wait, 0)

    width = coarse_in.shape[2]
    if share == 1:

        def coarse_load(g, j, lt):
            return crecv[4 * g + j, lt]

        def coarse_store(i, lt, real, imag):
            coarse_in[i, 0:16, lane_tile(lt)] = real
            coarse_in[i, 16:32, lane_tile(lt)] = imag

        def coarse_factor(s, c, lt):
            return coarse_tr[s, c:c + 1, lane_tile(lt)]

    else:
        turn = lax.rem(LANES - lax.rem(me, share) * width, LANES)

        def coarse_load(g, j, lt):
            return pltpu.roll(crecv[4 * g + j, lt].astype(F32), turn, 1)[:, :width]

        def coarse_store(i, lt, real, imag):
            coarse_in[i, 0:16, :] = real
            coarse_in[i, 16:32, :] = imag

        def coarse_factor(s, c, lt):
            return coarse_tr[s, c:c + 1, :]

    translate(n // 4, ctiles, coarse_load, coarse_mask, coarse_factor, coarse_store)

    each_mid(lambda c: c.wait_send())

    @pl.when(me < n - 1)
    def _():
        fine_copy(True).wait_send()

    @pl.when(me > 0)
    def _():
        fine_copy(False).wait_send()

    def sent(j, _):
        dest = lax.rem(me + 1 + j, n)
        coarse_copy(lax.div(dest, share), dest).wait_send()
        return 0

    lax.fori_loop(0, n - 1, sent, 0)


def local(
    nb, nd,
    fine_out, fine_list, fine_slot, fine_translator, theta_up_fine, phi_up_fine, middle_phase,
    middle_list, middle_slot, middle_translator, theta_up_middle, phi_up_middle, coarse_phase,
    coarse_list, coarse_translator,
):
    n = nb * nd
    b, d = lax.axis_index("box"), lax.axis_index("dir")
    held, comps, fine_dirs = fine_out.shape
    fine_mask = presence(fine_list, (b * nd + d) * held)
    mid_mask = presence(middle_list, b * middle_list.shape[0])
    coarse_mask = presence(coarse_list, 0)
    t_mid, q_mid = theta_up_fine.shape[0], phi_up_fine.shape[0]
    t_coarse, q_coarse = theta_up_middle.shape[0], phi_up_middle.shape[0]
    mid_phase = middle_phase.reshape(4, t_mid, q_mid)
    mid_phase = jnp.concatenate([mid_phase, mid_phase], axis=-1)
    co_phase = coarse_phase.reshape(4, t_coarse, q_coarse)
    mid_tiles = t_mid * q_mid // LANES
    width = coarse_translator.shape[2]
    ctiles = max(1, width // LANES)
    vmem = pl.BlockSpec(memory_space=pltpu.VMEM)
    smem = pl.BlockSpec(memory_space=pltpu.SMEM)
    dma = pltpu.SemaphoreType.DMA
    return pl.pallas_call(
        functools.partial(kernel, nb, nd),
        out_shape=(
            jax.ShapeDtypeStruct(fine_out.shape, BF16),
            jax.ShapeDtypeStruct((middle_list.shape[0], comps, middle_translator.shape[2]), BF16),
            jax.ShapeDtypeStruct((coarse_list.shape[0], comps, width), BF16),
        ),
        in_specs=[
            pl.BlockSpec(memory_space=pl.ANY), smem, smem, vmem, vmem, vmem, vmem,
            smem, smem, vmem, vmem, vmem, vmem, smem, vmem,
        ],
        out_specs=(vmem, vmem, vmem),
        scratch_shapes=[
            pltpu.VMEM((held + 8, comps, fine_dirs), BF16),
            pltpu.VMEM((mid_tiles, 4, comps, LANES), BF16),
            pltpu.VMEM((nd + 2, mid_tiles // nd, 4, comps, LANES), BF16),
            pltpu.VMEM((t_coarse, comps, LANES), BF16),
            pltpu.VMEM((n + 8, ctiles, comps, LANES), BF16),
            pltpu.VMEM((theta_up_fine.shape[1], held // 2 * comps, LANES), BF16),
            pltpu.VMEM((held // 2, t_mid, 16, 2 * LANES), F32),
            pltpu.VMEM((theta_up_middle.shape[1], 4 * comps, LANES), F32),
            pltpu.VMEM((8, t_coarse, 8, 2 * LANES), F32),
            pltpu.VMEM((held // 2, t_mid, LANES), F32),
            pltpu.VMEM((held // 2, t_mid, LANES), F32),
            pltpu.VMEM((4, t_coarse, LANES), F32),
            pltpu.VMEM((4, t_coarse, LANES), F32),
            dma, dma((2,)), dma((2,)), dma((2 * nd,)), dma((nd + 2,)), dma((n,)), dma((n,)),
        ],
        compiler_params=pltpu.CompilerParams(
            collective_id=0, has_side_effects=True, vmem_limit_bytes=48 * 1024 * 1024
        ),
        cost_estimate=pl.CostEstimate(
            flops=4_000_000_000, bytes_accessed=4_000_000, transcendentals=0
        ),
    )(
        fine_out, fine_mask, fine_slot, fine_translator, theta_up_fine, phi_up_fine, mid_phase,
        mid_mask, middle_slot, middle_translator, theta_up_middle, phi_up_middle, co_phase,
        coarse_mask, coarse_translator,
    )


def solution(mesh):
    return jax.shard_map(
        functools.partial(local, mesh.shape["box"], mesh.shape["dir"]),
        mesh=mesh,
        in_specs=(
            P(("box", "dir"), None, None),
            P(("box", "dir"), None),
            P("box"),
            P(),
            P(),
            P(),
            P(),
            P("box", None),
            P("box"),
            P(None, None, "dir"),
            P(),
            P(),
            P(),
            P(),
            P(None, None, ("box", "dir")),
        ),
        out_specs=(
            P(("box", "dir"), None, None),
            P("box", None, "dir"),
            P(None, None, ("box", "dir")),
        ),
        check_vma=False,
    )
```

time: 208 us -> 45.7 us (0.22); the launches traced: 205 us -> 45.1 us
  other arithmetic: 85.1 us -> 3.59 us
  local copies, waits for them, and re-layouts: 73.2 us -> 8.34 us
  Pallas kernels: 0 us -> 32.4 us
  starting transfers between devices: 25.6 us -> 0 us
  matrix products: 11.5 us -> 0 us
  waiting for transfers between devices: 6.88 us -> 0 us
    unnamed x1 -> x0, other arithmetic: 45.2 us -> none
    pallas_call x0 -> x1, Pallas kernels: none -> 32.4 us  [local(): pl.pallas_call(functools.partial(kernel, nb, nd), out_shape=(jax.ShapeDty...]
    another operation x6 -> x0, other arithmetic: 19.3 us -> none
    all_to_all x3 -> x0, starting transfers between devices: 14.9 us -> none  [the longest x1 5.68 us: local(): lax.all_to_all(coarse_own, 'box', split_axis=2, concat_axis=0, tiled=True)]
    reshape x3 -> x1, local copies, waits for them, and re-layouts: 15.5 us -> 0.87 us  [local(): mid_phase = middle_phase.reshape(4, t_mid, q_mid)]
    all_to_all x5 -> x0, local copies, waits for them, and re-layouts: 14.3 us -> none  [the longest x3 9.79 us: local(): lax.all_to_all(coarse_own, 'box', split_axis=2, concat_axis=0, tiled=True)]
    unnamed x177 -> x20, local copies, waits for them, and re-layouts: 21 us -> 7.2 us
    dot_general x7 -> x0, matrix products: 11.5 us -> none  [the longest x2 5.92 us: interpolate(): jnp.einsum('naq,ta->ntq', along_phi, theta_matrix, preferred_element_type...]
  transfers between devices with their start and end apart: 7 -> 0, of which waited for: 3 -> 0; matrix products, arithmetic and copies ran while one was open for 53% -> 0% of each run, Pallas kernels for 0% -> 0%
where the time goes in v1:
time: 45.7 us; the launch traced here: 45.1 us
  Pallas kernels  32.4 us (71%)
  local copies, waits for them, and re-layouts  8.34 us (18%)
  other arithmetic  3.59 us (8%)
  between operations  0.77 us (2%)
    pallas_call x1, Pallas kernels, local(): pl.pallas_call(functools.partial(kernel, nb, nd), out_shape=(jax.ShapeDty...  32.4 us
    unnamed x20, local copies, waits for them, and re-layouts  7.2 us
    reduce_or x2, other arithmetic, presence(): jnp.any(entries[:, None, :] == wanted[:, :, None], axis=2).astype(F32)  2.03 us
    add x2, other arithmetic, presence(): wanted = ids[:, None] + jnp.array(offsets_used(), jnp.int32)[None, :]  1.45 us

profile of v1, /device:TPU:11, one launch (start us, length us, event | category | flops | bytes accessed | tf_op | source)
XLA Modules:
  0.0 45.1 jit_solution(8855173606994523285)
XLA Ops:
  0.6 0.0 copy-start
  0.7 0.8 %copy.35.theta_f = bf16[32,16]{1,0:T(8,128)(2,1)S(1)} copy(bf16[32,16]{0,1:T(8,128)(2,1)} %param.22) | data formatting | bytes 2048 | tf_op args[4]
  1.5 0.7 %iota_add_fusion = s32[32,12]{0,1:T(8,128)S(1)} fusion(s32[12]{0:T(128)} %constant.17.clone), kind=kLoop, calls=%fused_computation.5 | loop fusion | flops 384 | bytes 1584 | tf_op jit(solution)/shard_map/add | solution.py:23
  2.2 0.7 %compare_reduce_fusion = pred[32,12]{0,1:T(8,128)(4,1)S(1)} fusion(s32[32,12]{0,1:T(8,128)S(1)} %iota_add_fusion, s32[32,12]{0,1:T(8,128)} %param.31), kind=kLoop, calls=%fused_computation.1 | loop fusion | flops 8832 | bytes 3456 | tf_op jit(solution)/shard_map/reduce_or | solution.py:24
  3.0 0.1 copy.39.coarse_mask
  3.1 0.7 %broadcast_add_fusion = (s32[16,12]{0,1:T(8,128)S(1)}, s32[16,12]{0,1:T(8,128)S(1)}) fusion(s32[16]{0:T(128)S(1)} %iota_add_fusion.1, s32[12]{0:T(128)} %constant.17.clone, s32[16]{0:T(128)S(1)} %iota_add_fusion.2), kind=kLoop, calls=%fused_computation.6 | loop fusion | flops 384 | bytes 1712 | tf_op jit(solution)/shard_map/add | solution.py:23
  3.8 1.3 %compare_reduce_fusion.1 = (pred[16,12]{0,1:T(8,128)(4,1)S(1)}, pred[16,12]{0,1:T(8,128)(4,1)S(1)}) fusion(s32[16,12]{0,1:T(8,128)S(1)} %get-tuple-element.3, s32[16,12]{1,0:T(8,128)} %param.25, s32[16,12]{0,1:T(8,128)S(1)} %get-tuple-element.4, s32[16,12]{1,0:T(8,128)} %param.19), kind=kLoop, calls=%fused_computation.2 | loop fusion | flops 8832 | bytes 3456 | tf_op jit(solution)/shard_map/reduce_or | solution.py:24
  5.1 0.1 copy.34
  5.2 0.1 copy.33
  5.3 0.8 %copy.36.phi_f = bf16[64,32]{1,0:T(8,128)(2,1)S(1)} copy(bf16[64,32]{0,1:T(8,128)(2,1)} %param.23) | data formatting | bytes 8192 | tf_op args[5]
  6.1 0.8 %copy.37.theta_m = bf16[64,32]{1,0:T(8,128)(2,1)S(1)} copy(bf16[64,32]{0,1:T(8,128)(2,1)} %param.28) | data formatting | bytes 8192 | tf_op args[10]
  6.9 0.8 %copy.38.phi_m = bf16[128,64]{1,0:T(8,128)(2,1)S(1)} copy(bf16[128,64]{0,1:T(8,128)(2,1)} %param.29) | data formatting | bytes 32768 | tf_op args[11]
  7.7 0.9 %reshape.93 = f32[4,32,64]{2,1,0:T(8,128)S(1)} reshape(f32[4,2048]{1,0:T(4,128)} %param.24) | data formatting | bytes 65536 | tf_op jit(solution)/shard_map/reshape | solution.py:462
  8.6 0.1 pad_maximum_fusion.mid_phase
  8.7 0.0 copy-start.1
  8.7 0.0 copy-start.2
  8.7 0.0 copy-start.3
  8.7 0.9 %copy.42 = f32[1,4,64,128]{3,2,1,0:T(8,128)S(1)} copy(f32[1,4,64,128]{3,1,2,0:T(4,128)} %bitcast.5) | data formatting | bytes 262144
  9.6 0.0 copy-start.4
  9.6 0.0 copy-start.5
  9.7 0.0 copy-done
  9.7 0.0 copy-done.1
  9.7 0.0 copy-done.2
  9.7 0.0 copy-done.3
  9.7 0.6 %copy-done.4 = s32[64]{0:T(128)S(1)} copy-done((s32[64]{0:T(128)S(1)}, s32[64]{0:T(128)}, u32[]{:S(2)}) %copy-start.4) | copy-done | bytes 280
  10.3 0.0 copy-done.5
  10.3 32.4 %shard_map.193 = (bf16[16,32,512]{2,1,0:T(8,128)(2,1)S(1)}, bf16[16,32,512]{2,1,0:T(8,128)(2,1)S(1)}, bf16[32,32,256]{2,1,0:T(8,128)(2,1)S(1)}) custom-call(bf16[16,32,512]{2,1,0:T(8,128)(2,1)S(1)} %copy-done, f32[16,12]{1,0:T(8,128)S(1)} %convert_element_type.9.fine_mask, s32[64]{0:T(128)S(1)} %copy-done.4, f32[12,2,512]{2,1,0:T(2,128)S(1)} %copy-done.1, ...), custom_call_target="tpu_custom_call" | custom-call | flops 4000000000 | bytes 4000000 | tf_op jit(solution)/shard_map/pallas_call | solution.py:471
  42.7 0.8 %copy.46 = bf16[16,32,512]{2,1,0:T(8,128)(2,1)} copy(bf16[16,32,512]{2,1,0:T(8,128)(2,1)S(1)} %get-tuple-element.10) | data formatting | bytes 1048576
  43.5 0.8 %copy.47 = bf16[16,32,512]{2,1,0:T(8,128)(2,1)} copy(bf16[16,32,512]{2,1,0:T(8,128)(2,1)S(1)} %get-tuple-element.11) | data formatting | bytes 1048576
  44.3 0.8 %copy.48 = bf16[32,32,256]{2,1,0:T(8,128)(2,1)} copy(bf16[32,32,256]{2,1,0:T(8,128)(2,1)S(1)} %get-tuple-element.12) | data formatting | bytes 1048576
  (5 shorter events, 0.0 us)
Async XLA Ops:
  0.6 9.0 %copy-start = (bf16[16,32,512]{2,1,0:T(8,128)(2,1)S(1)}, bf16[16,32,512]{2,1,0:T(8,128)(2,1)}, u32[]{:S(2)}) copy-start(bf16[16,32,512]{2,1,0:T(8,128)(2,1)} %fine_hbm.1) | copy-start | bytes 1572868
  8.7 1.0 %copy-start.1 = (f32[12,2,512]{2,1,0:T(2,128)S(1)}, f32[12,2,512]{2,1,0:T(2,128)}, u32[]{:S(2)}) copy-start(f32[12,2,512]{2,1,0:T(2,128)} %fine_tr.1) | copy-start | bytes 147460
  8.7 1.0 %copy-start.2 = (f32[12,2,512]{2,1,0:T(2,128)S(1)}, f32[12,2,512]{2,1,0:T(2,128)}, u32[]{:S(2)}) copy-start(f32[12,2,512]{2,1,0:T(2,128)} %mid_tr.1) | copy-start | bytes 147460
  8.7 1.0 %copy-start.3 = (f32[12,2,256]{2,1,0:T(2,128)S(1)}, f32[12,2,256]{2,1,0:T(2,128)}, u32[]{:S(2)}) copy-start(f32[12,2,256]{2,1,0:T(2,128)} %coarse_tr.1) | copy-start | bytes 73732
  9.6 0.7 %copy-start.4 = (s32[64]{0:T(128)S(1)}, s32[64]{0:T(128)}, u32[]{:S(2)}) copy-start(s32[64]{0:T(128)} %fine_slot.1) | copy-start | bytes 772
  9.6 0.7 %copy-start.5 = (s32[16]{0:T(128)S(1)}, s32[16]{0:T(128)}, u32[]{:S(2)}) copy-start(s32[16]{0:T(128)} %mid_slot.1) | copy-start | bytes 196

commit v2 on v1

--- a/solution.py
+++ b/solution.py
@@ -18,12 +18,6 @@
     return list(range(-MAX_OFFSET, -1)) + list(range(2, MAX_OFFSET + 1))
 
 
-def presence(entries, first_box):
-    ids = first_box + jnp.arange(entries.shape[0], dtype=jnp.int32)
-    wanted = ids[:, None] + jnp.array(offsets_used(), jnp.int32)[None, :]
-    return jnp.any(entries[:, None, :] == wanted[:, :, None], axis=2).astype(F32)
-
-
 def iota(shape, dim):
     return lax.broadcasted_iota(jnp.int32, shape, dim)
 
@@ -37,23 +31,23 @@
 
 
 def kron_identity(matrix, width):
-    rows, cols = matrix.shape
+    cols, rows = matrix.shape
     shift = width.bit_length() - 1
     left = one_hot((iota((rows * width, rows), 0) >> shift) == iota((rows * width, rows), 1))
     right = one_hot(iota((cols, cols * width), 0) == (iota((cols, cols * width), 1) >> shift))
-    full = dot(dot(left, matrix).astype(BF16), right)
+    full = dot(dot(left, matrix, ((1,), (1,))).astype(BF16), right)
     shape = (rows * width, cols * width)
     keep = (iota(shape, 0) & (width - 1)) == (iota(shape, 1) & (width - 1))
     return jnp.where(keep, full, 0.0).astype(BF16)
 
 
 def phi_blocks(phi, pair):
-    q, p = phi.shape
+    p, q = phi.shape
     thetas = 256 // (pair * p)
     rows, cols = pair * thetas * p, thetas * pair * q
     left = one_hot((iota((rows, p), 0) & (p - 1)) == iota((rows, p), 1))
     right = one_hot(iota((q, cols), 0) == (iota((q, cols), 1) & (q - 1)))
-    full = dot(dot(left, phi, ((1,), (1,))).astype(BF16), right)
+    full = dot(dot(left, phi).astype(BF16), right)
     shape = (rows, cols)
     r, c = iota(shape, 0), iota(shape, 1)
     ps, qs = p.bit_length() - 1, q.bit_length() - 1
@@ -63,23 +57,58 @@
     return jnp.where((row_t == col_t) & (row_h == col_h), full, 0.0).astype(BF16)
 
 
+def spread(mask, s, column):
+    rows = column.shape[0]
+    mask[s] = jnp.broadcast_to(column[:, :, None], (rows, 8, LANES))
+
+
+def row_presence(mask, entries, first_box):
+    ids = first_box + iota(entries.shape, 0)
+    for s, offset in enumerate(offsets_used()):
+        hit = jnp.where(entries == ids + offset, 1.0, 0.0)
+        spread(mask, s, jnp.max(hit, axis=1, keepdims=True))
+
+
+def column_presence(mask, entries):
+    count = entries.shape[1]
+    ids = iota(entries.shape, 1)
+    eye = iota((count, count), 0) == iota((count, count), 1)
+    for s, offset in enumerate(offsets_used()):
+        hit = jnp.where(entries == ids + offset, 1.0, 0.0)
+        row = jnp.max(hit, axis=0, keepdims=True)
+        spread(mask, s, jnp.sum(jnp.where(eye, row, 0.0), axis=1, keepdims=True))
+
+
+def repeat_rows(wide, factors):
+    for s in range(factors.shape[0]):
+        for c in range(2):
+            wide[s, c] = jnp.broadcast_to(factors[s, c:c + 1, :], wide.shape[2:])
+
+
+def pack_rows(table):
+    half = table.shape[0] // 2
+    return jnp.concatenate([table[:half], table[half:]], axis=1)
+
+
 def translate(groups, tiles, load, mask_ref, factor, store):
     def step(it, _):
         g, lt = lax.div(it, tiles), lax.rem(it, tiles)
         sources = [load(g, j, lt).astype(F32) for j in range(12)]
-        half = sources[0].shape[0] // 2
+        sources = [x.reshape(4, 8, x.shape[1]) for x in sources]
+        width = sources[0].shape[2]
         for i in range(4):
             real, imag = None, None
             for s, offset in enumerate(offsets_used()):
                 j = 4 + i + offset
                 if j < 0 or j > 11:
                     continue
-                m = mask_ref[4 * g + i, s]
+                m = mask_ref[s, 4 * g + i][:, :width]
                 a, b = factor(s, 0, lt) * m, factor(s, 1, lt) * m
-                pr, pi = sources[j][:half], sources[j][half:]
+                pr, pi = sources[j][:2], sources[j][2:]
                 tr, ti = a * pr - b * pi, a * pi + b * pr
                 real = tr if real is None else real + tr
                 imag = ti if imag is None else imag + ti
+            real, imag = real.reshape(16, width), imag.reshape(16, width)
             store(4 * g + i, lt, real.astype(BF16), imag.astype(BF16))
         return 0
 
@@ -92,18 +121,18 @@
 
 def kernel(
     nb, nd,
-    fine_hbm, fine_mask, fine_slot, fine_tr, theta_f, phi_f, mid_phase,
-    mid_mask, mid_slot, mid_tr, theta_m, phi_m, coarse_phase, coarse_mask, coarse_tr,
+    fine_hbm, fine_list, fine_slot, fine_tr, theta_f, phi_f, mid_phase,
+    mid_list, mid_slot, mid_tr, theta_m, phi_m, coarse_phase, coarse_list, coarse_tr,
     fine_in, mid_in, coarse_in,
     fpad, par, mrecv, crs, crecv, along1, lift1, along2, lift2,
-    cosm, sinm, cosc, sinc,
+    cosm, sinm, cosc, sinc, fine_mask, mid_mask, coarse_mask, fine_wide, mid_wide, coarse_wide,
     load_sem, fsend, frecv, msend, mrecv_sem, csend, crecv_sem,
 ):
     n = nb * nd
     b, d = lax.axis_index("box"), lax.axis_index("dir")
     me = b * nd + d
     held = fine_in.shape[0]
-    t_mid, t_coarse = theta_f.shape[0], theta_m.shape[0]
+    t_mid, t_coarse = theta_f.shape[1], theta_m.shape[1]
     mid_tiles = par.shape[0]
     mlt = mid_tiles // nd
     ctiles = crecv.shape[1]
@@ -129,21 +158,22 @@
     k1 = kron_identity(theta_f[...], 16)
     bd2 = phi_blocks(phi_m[...], 1)
     k2 = kron_identity(theta_m[...], 8)
-    cosc[...] = jnp.cos(coarse_phase[...])
-    sinc[...] = jnp.sin(coarse_phase[...])
-    cosine, sine = jnp.cos(mid_phase[...]), jnp.sin(mid_phase[...])
-    low = iota((t_mid, LANES), 1) < LANES // 2
-    for u in range(2):
-        for k in range(4):
-            s0 = fine_slot[d * held + 8 * u + k]
-            s1 = fine_slot[d * held + 8 * u + 4 + k]
-            for table, values in ((cosm, cosine), (sinm, sine)):
-                first = values[3]
-                second = values[3]
-                for s in range(3):
-                    first = jnp.where(s0 == s, values[s], first)
-                    second = jnp.where(s1 == s, values[s], second)
-                table[4 * u + k] = jnp.where(low, first, second)
+    angles = pack_rows(coarse_phase[...])
+    cosc[...] = jnp.cos(angles)
+    sinc[...] = jnp.sin(angles)
+    angles = pack_rows(mid_phase[...])
+    low8 = iota(angles.shape, 2) < LANES // 2
+    for table, values in ((cosm, jnp.cos(angles)), (sinm, jnp.sin(angles))):
+        turned = pltpu.roll(values, LANES // 2, 2)
+        table[0] = jnp.where(low8, values, turned)
+        table[1] = jnp.where(low8, turned, values)
+    fine_slots = [fine_slot[d * held + c] for c in range(held)]
+    row_presence(fine_mask, fine_list[...], me * held)
+    row_presence(mid_mask, mid_list[...], b * mid_list.shape[0])
+    column_presence(coarse_mask, coarse_list[...])
+    repeat_rows(fine_wide, fine_tr)
+    repeat_rows(mid_wide, mid_tr)
+    repeat_rows(coarse_wide, coarse_tr)
 
     zeros4 = jnp.zeros((4,) + fpad.shape[1:], BF16)
 
@@ -187,7 +217,17 @@
 
     lower = iota((16, LANES), 1) < LANES // 2
 
+    low1 = iota((1, LANES), 1) < LANES // 2
+    half_mid = mid_tiles // 2
+
     def parents_step(v, _):
+        place, step4 = lax.rem(v, half_mid), 4 * lax.div(v, half_mid)
+
+        def phase_row(table, e, u, k):
+            first = table[e, place, pl.ds(fine_slots[8 * u + k] + step4, 1), :]
+            second = table[e, place, pl.ds(fine_slots[8 * u + 4 + k] + step4, 1), :]
+            return jnp.where(low1, first, second)
+
         for u in range(2):
             sums = []
             for e in range(2):
@@ -197,8 +237,8 @@
                     uk = 4 * u + k
                     value = lift1[uk, t2]
                     vr, vi = value[:, :LANES], value[:, LANES:]
-                    co = cosm[uk, pl.ds(t2, 1), :]
-                    si = sinm[uk, pl.ds(t2, 1), :]
+                    co = phase_row(cosm, e, u, k)
+                    si = phase_row(sinm, e, u, k)
                     tr, ti = co * vr - si * vi, co * vi + si * vr
                     real = tr if real is None else real + tr
                     imag = ti if imag is None else imag + ti
@@ -307,13 +347,14 @@
     my_tile = lax.div(me, share)
 
     def coarse_step(j, _):
-        tile = lax.rem(my_tile + 1 + j, ntile)
+        tile = lax.rem(my_tile + ntile // 4 + j, ntile)
         for i in range(ctiles):
             t2 = tile * ctiles + i
             reals, imags = [None, None], [None, None]
             for k in range(4):
-                co = cosc[slots[k], pl.ds(t2, 1), :]
-                si = sinc[slots[k], pl.ds(t2, 1), :]
+                row = pl.ds(slots[k] + 4 * lax.div(t2, t_coarse // 2), 1)
+                co = cosc[lax.rem(t2, t_coarse // 2), row, :]
+                si = sinc[lax.rem(t2, t_coarse // 2), row, :]
                 for cg in range(2):
                     value = lift2[2 * k + cg, t2]
                     vr, vi = value[:, :LANES], value[:, LANES:]
@@ -351,7 +392,7 @@
         fine_in.shape[2] // LANES,
         lambda g, j, lt: fpad[4 * g + j, :, lane_tile(lt)],
         fine_mask,
-        lambda s, c, lt: fine_tr[s, c:c + 1, lane_tile(lt)],
+        lambda s, c, lt: fine_wide[s, c, :, lane_tile(lt)],
         fine_store,
     )
 
@@ -381,7 +422,7 @@
         mlt,
         lambda g, j, lt: mrecv[g + j // 4, lt, j % 4],
         mid_mask,
-        lambda s, c, lt: mid_tr[s, c:c + 1, lane_tile(lt)],
+        lambda s, c, lt: mid_wide[s, c, :, lane_tile(lt)],
         mid_store,
     )
 
@@ -410,7 +451,7 @@
             coarse_in[i, 16:32, lane_tile(lt)] = imag
 
         def coarse_factor(s, c, lt):
-            return coarse_tr[s, c:c + 1, lane_tile(lt)]
+            return coarse_wide[s, c, :, lane_tile(lt)]
 
     else:
         turn = lax.rem(LANES - lax.rem(me, share) * width, LANES)
@@ -423,7 +464,7 @@
             coarse_in[i, 16:32, :] = imag
 
         def coarse_factor(s, c, lt):
-            return coarse_tr[s, c:c + 1, :]
+            return coarse_wide[s, c]
 
     translate(n // 4, ctiles, coarse_load, coarse_mask, coarse_factor, coarse_store)
 
@@ -452,18 +493,14 @@
     coarse_list, coarse_translator,
 ):
     n = nb * nd
-    b, d = lax.axis_index("box"), lax.axis_index("dir")
     held, comps, fine_dirs = fine_out.shape
-    fine_mask = presence(fine_list, (b * nd + d) * held)
-    mid_mask = presence(middle_list, b * middle_list.shape[0])
-    coarse_mask = presence(coarse_list, 0)
     t_mid, q_mid = theta_up_fine.shape[0], phi_up_fine.shape[0]
-    t_coarse, q_coarse = theta_up_middle.shape[0], phi_up_middle.shape[0]
-    mid_phase = middle_phase.reshape(4, t_mid, q_mid)
-    mid_phase = jnp.concatenate([mid_phase, mid_phase], axis=-1)
-    co_phase = coarse_phase.reshape(4, t_coarse, q_coarse)
+    t_coarse = theta_up_middle.shape[0]
+    mid_phase = middle_phase.reshape(4, -1, LANES).transpose(1, 0, 2)
+    co_phase = coarse_phase.reshape(4, -1, LANES).transpose(1, 0, 2)
     mid_tiles = t_mid * q_mid // LANES
     width = coarse_translator.shape[2]
+    slots = fine_list.shape[1]
     ctiles = max(1, width // LANES)
     vmem = pl.BlockSpec(memory_space=pltpu.VMEM)
     smem = pl.BlockSpec(memory_space=pltpu.SMEM)
@@ -476,8 +513,8 @@
             jax.ShapeDtypeStruct((coarse_list.shape[0], comps, width), BF16),
         ),
         in_specs=[
-            pl.BlockSpec(memory_space=pl.ANY), smem, smem, vmem, vmem, vmem, vmem,
-            smem, smem, vmem, vmem, vmem, vmem, smem, vmem,
+            pl.BlockSpec(memory_space=pl.ANY), vmem, smem, vmem, vmem, vmem, vmem,
+            vmem, smem, vmem, vmem, vmem, vmem, vmem, vmem,
         ],
         out_specs=(vmem, vmem, vmem),
         scratch_shapes=[
@@ -490,10 +527,16 @@
             pltpu.VMEM((held // 2, t_mid, 16, 2 * LANES), F32),
             pltpu.VMEM((theta_up_middle.shape[1], 4 * comps, LANES), F32),
             pltpu.VMEM((8, t_coarse, 8, 2 * LANES), F32),
-            pltpu.VMEM((held // 2, t_mid, LANES), F32),
-            pltpu.VMEM((held // 2, t_mid, LANES), F32),
-            pltpu.VMEM((4, t_coarse, LANES), F32),
-            pltpu.VMEM((4, t_coarse, LANES), F32),
+            pltpu.VMEM((2, mid_tiles // 2, 8, LANES), F32),
+            pltpu.VMEM((2, mid_tiles // 2, 8, LANES), F32),
+            pltpu.VMEM((t_coarse // 2, 8, LANES), F32),
+            pltpu.VMEM((t_coarse // 2, 8, LANES), F32),
+            pltpu.VMEM((slots, held, 8, LANES), F32),
+            pltpu.VMEM((slots, middle_list.shape[0], 8, LANES), F32),
+            pltpu.VMEM((slots, coarse_list.shape[0], 8, LANES), F32),
+            pltpu.VMEM((slots, 2, 8, fine_dirs), F32),
+            pltpu.VMEM((slots, 2, 8, middle_translator.shape[2]), F32),
+            pltpu.VMEM((slots, 2, 8, width), F32),
             dma, dma((2,)), dma((2,)), dma((2 * nd,)), dma((nd + 2,)), dma((n,)), dma((n,)),
         ],
         compiler_params=pltpu.CompilerParams(
@@ -503,9 +546,9 @@
             flops=4_000_000_000, bytes_accessed=4_000_000, transcendentals=0
         ),
     )(
-        fine_out, fine_mask, fine_slot, fine_translator, theta_up_fine, phi_up_fine, mid_phase,
-        mid_mask, middle_slot, middle_translator, theta_up_middle, phi_up_middle, co_phase,
-        coarse_mask, coarse_translator,
+        fine_out, fine_list, fine_slot, fine_translator, theta_up_fine.T, phi_up_fine.T, mid_phase,
+        middle_list, middle_slot, middle_translator, theta_up_middle.T, phi_up_middle.T, co_phase,
+        coarse_list.T, coarse_translator,
     )
 
 

time: 45.7 us -> 44.6 us (0.976)
  other arithmetic: 3.59 us -> 0 us
  local copies, waits for them, and re-layouts: 8.34 us -> 11.6 us
  Pallas kernels: 32.4 us -> 31.6 us
    unnamed x20 -> x33, local copies, waits for them, and re-layouts: 7.2 us -> 11.6 us
    reduce_or x2 -> x0, other arithmetic: 2.03 us -> none  [presence(): jnp.any(entries[:, None, :] == wanted[:, :, None], axis=2).astype(F32)]
    add x4 -> x0, other arithmetic: 1.46 us -> none  [the longest x2 1.45 us: presence(): wanted = ids[:, None] + jnp.array(offsets_used(), jnp.int32)[None, :]]
    reshape x1 -> x0, local copies, waits for them, and re-layouts: 0.87 us -> none  [local(): mid_phase = middle_phase.reshape(4, t_mid, q_mid)]
    pallas_call x1, Pallas kernels: 32.4 us -> 31.6 us  [local(): pl.pallas_call(functools.partial(kernel, nb, nd), out_shape=(jax.ShapeDty...]
where the time goes in v2:
time: 44.6 us; the launch traced here: 43.9 us
  Pallas kernels  31.6 us (71%)
  local copies, waits for them, and re-layouts  11.6 us (26%)
  between operations  0.69 us (2%)
    pallas_call x1, Pallas kernels, local(): pl.pallas_call(functools.partial(kernel, nb, nd), out_shape=(jax.ShapeDty...  31.6 us
    unnamed x33, local copies, waits for them, and re-layouts  11.6 us

profile of v2, /device:TPU:11, one launch (start us, length us, event | category | flops | bytes accessed | tf_op | source)
XLA Modules:
  0.0 43.9 jit_solution(10462693433768027861)
XLA Ops:
  0.6 0.0 copy-start.7
  0.6 0.0 copy-start.12
  0.7 0.0 copy-start.13
  0.7 0.0 copy-start.14
  0.7 0.7 %copy-done.7 = s32[16,12]{1,0:T(8,128)S(1)} copy-done((s32[16,12]{1,0:T(8,128)S(1)}, s32[16,12]{1,0:T(8,128)}, u32[]{:S(2)}) %copy-start.7) | copy-done | bytes 792
  1.3 0.0 copy-done.12
  1.3 0.0 copy-done.13
  1.3 0.0 copy-done.14
  1.3 0.0 copy-start
  1.3 1.0 %copy-done = bf16[16,32,512]{2,1,0:T(8,128)(2,1)S(1)} copy-done((bf16[16,32,512]{2,1,0:T(8,128)(2,1)S(1)}, bf16[16,32,512]{2,1,0:T(8,128)(2,1)}, u32[]{:S(2)}) %copy-start) | copy-done | bytes 524312
  2.4 0.0 copy-start.1
  2.4 0.9 %copy-done.1 = f32[4,8192]{1,0:T(4,128)S(1)} copy-done((f32[4,8192]{1,0:T(4,128)S(1)}, f32[4,8192]{1,0:T(4,128)}, u32[]{:S(2)}) %copy-start.1) | copy-done | bytes 131096
  3.3 0.0 copy-start.2
  3.3 0.8 %copy-done.2 = f32[12,2,512]{2,1,0:T(2,128)S(1)} copy-done((f32[12,2,512]{2,1,0:T(2,128)S(1)}, f32[12,2,512]{2,1,0:T(2,128)}, u32[]{:S(2)}) %copy-start.2) | copy-done | bytes 49176
  4.1 0.0 copy-start.3
  4.1 0.8 %copy-done.3 = f32[12,2,512]{2,1,0:T(2,128)S(1)} copy-done((f32[12,2,512]{2,1,0:T(2,128)S(1)}, f32[12,2,512]{2,1,0:T(2,128)}, u32[]{:S(2)}) %copy-start.3) | copy-done | bytes 49176
  4.9 0.0 copy-start.4
  4.9 0.8 %copy-done.4 = f32[4,2048]{1,0:T(4,128)S(1)} copy-done((f32[4,2048]{1,0:T(4,128)S(1)}, f32[4,2048]{1,0:T(4,128)}, u32[]{:S(2)}) %copy-start.4) | copy-done | bytes 32792
  5.7 0.0 copy-start.5
  5.7 0.7 %copy-done.5 = f32[12,2,256]{2,1,0:T(2,128)S(1)} copy-done((f32[12,2,256]{2,1,0:T(2,128)S(1)}, f32[12,2,256]{2,1,0:T(2,128)}, u32[]{:S(2)}) %copy-start.5) | copy-done | bytes 24600
  6.4 0.7 %copy-done.6 = bf16[128,64]{0,1:T(8,128)(2,1)S(1)} copy-done((bf16[128,64]{0,1:T(8,128)(2,1)S(1)}, bf16[128,64]{0,1:T(8,128)(2,1)}, u32[]{:S(2)}) %copy-start.6) | copy-done | bytes 16408
  7.1 0.0 copy-start.8
  7.1 0.7 %copy-done.8 = bf16[64,32]{0,1:T(8,128)(2,1)S(1)} copy-done((bf16[64,32]{0,1:T(8,128)(2,1)S(1)}, bf16[64,32]{0,1:T(8,128)(2,1)}, u32[]{:S(2)}) %copy-start.8) | copy-done | bytes 4120
  7.8 0.0 copy-start.9
  7.8 0.7 %copy-done.9 = s32[16,12]{1,0:T(8,128)S(1)} copy-done((s32[16,12]{1,0:T(8,128)S(1)}, s32[16,12]{1,0:T(8,128)}, u32[]{:S(2)}) %copy-start.9) | copy-done | bytes 792
  8.5 0.0 copy-start.10
  8.5 0.7 %copy-done.10 = bf16[64,32]{0,1:T(8,128)(2,1)S(1)} copy-done((bf16[64,32]{0,1:T(8,128)(2,1)S(1)}, bf16[64,32]{0,1:T(8,128)(2,1)}, u32[]{:S(2)}) %copy-start.10) | copy-done | bytes 4120
  9.2 0.7 %copy-done.11 = s32[32,12]{0,1:T(8,128)S(1)} copy-done((s32[32,12]{0,1:T(8,128)S(1)}, s32[32,12]{0,1:T(8,128)}, u32[]{:S(2)}) %copy-start.11) | copy-done | bytes 1560
  9.9 31.6 %shard_map.166 = (bf16[16,32,512]{2,1,0:T(8,128)(2,1)S(1)}, bf16[16,32,512]{2,1,0:T(8,128)(2,1)S(1)}, bf16[32,32,256]{2,1,0:T(8,128)(2,1)S(1)}) custom-call(bf16[16,32,512]{2,1,0:T(8,128)(2,1)S(1)} %copy-done, s32[16,12]{1,0:T(8,128)S(1)} %copy-done.7, s32[64]{0:T(128)S(1)} %copy-done.13, f32[12,2,512]{2,1,0:T(2,128)S(1)} %copy-done.2, ...), custom_call_target="tpu_custom_call" | custom-call | flops 4000000000 | bytes 4000000 | tf_op jit(solution)/shard_map/pallas_call | solution.py:508
  41.5 0.8 %copy.21 = bf16[16,32,512]{2,1,0:T(8,128)(2,1)} copy(bf16[16,32,512]{2,1,0:T(8,128)(2,1)S(1)} %get-tuple-element.6) | data formatting | bytes 1048576
  42.3 0.8 %copy.22 = bf16[16,32,512]{2,1,0:T(8,128)(2,1)} copy(bf16[16,32,512]{2,1,0:T(8,128)(2,1)S(1)} %get-tuple-element.7) | data formatting | bytes 1048576
  43.1 0.8 %copy.23 = bf16[32,32,256]{2,1,0:T(8,128)(2,1)} copy(bf16[32,32,256]{2,1,0:T(8,128)(2,1)S(1)} %get-tuple-element.8) | data formatting | bytes 1048576
  (2 shorter events, 0.0 us)
Async XLA Ops:
  0.6 0.7 %copy-start.7 = (s32[16,12]{1,0:T(8,128)S(1)}, s32[16,12]{1,0:T(8,128)}, u32[]{:S(2)}) copy-start(s32[16,12]{1,0:T(8,128)} %fine_list.1) | copy-start | bytes 2308
  0.6 0.7 %copy-start.12 = (bf16[32,16]{0,1:T(8,128)(2,1)S(1)}, bf16[32,16]{0,1:T(8,128)(2,1)}, u32[]{:S(2)}) copy-start(bf16[32,16]{0,1:T(8,128)(2,1)} %param.19) | copy-start | bytes 3076
  0.7 0.7 %copy-start.13 = (s32[64]{0:T(128)S(1)}, s32[64]{0:T(128)}, u32[]{:S(2)}) copy-start(s32[64]{0:T(128)} %fine_slot.1) | copy-start | bytes 772
  0.7 0.7 %copy-start.14 = (s32[16]{0:T(128)S(1)}, s32[16]{0:T(128)}, u32[]{:S(2)}) copy-start(s32[16]{0:T(128)} %mid_slot.1) | copy-start | bytes 196
  1.3 1.0 %copy-start = (bf16[16,32,512]{2,1,0:T(8,128)(2,1)S(1)}, bf16[16,32,512]{2,1,0:T(8,128)(2,1)}, u32[]{:S(2)}) copy-start(bf16[16,32,512]{2,1,0:T(8,128)(2,1)} %fine_hbm.1) | copy-start | bytes 1572868
  2.4 0.9 %copy-start.1 = (f32[4,8192]{1,0:T(4,128)S(1)}, f32[4,8192]{1,0:T(4,128)}, u32[]{:S(2)}) copy-start(f32[4,8192]{1,0:T(4,128)} %param.27) | copy-start | bytes 393220
  3.3 0.8 %copy-start.2 = (f32[12,2,512]{2,1,0:T(2,128)S(1)}, f32[12,2,512]{2,1,0:T(2,128)}, u32[]{:S(2)}) copy-start(f32[12,2,512]{2,1,0:T(2,128)} %fine_tr.1) | copy-start | bytes 147460
  4.1 0.8 %copy-start.3 = (f32[12,2,512]{2,1,0:T(2,128)S(1)}, f32[12,2,512]{2,1,0:T(2,128)}, u32[]{:S(2)}) copy-start(f32[12,2,512]{2,1,0:T(2,128)} %mid_tr.1) | copy-start | bytes 147460
  4.9 0.8 %copy-start.4 = (f32[4,2048]{1,0:T(4,128)S(1)}, f32[4,2048]{1,0:T(4,128)}, u32[]{:S(2)}) copy-start(f32[4,2048]{1,0:T(4,128)} %param.21) | copy-start | bytes 98308
  5.7 0.7 %copy-start.5 = (f32[12,2,256]{2,1,0:T(2,128)S(1)}, f32[12,2,256]{2,1,0:T(2,128)}, u32[]{:S(2)}) copy-start(f32[12,2,256]{2,1,0:T(2,128)} %coarse_tr.1) | copy-start | bytes 73732
  6.4 0.7 %copy-start.6 = (bf16[128,64]{0,1:T(8,128)(2,1)S(1)}, bf16[128,64]{0,1:T(8,128)(2,1)}, u32[]{:S(2)}) copy-start(bf16[128,64]{0,1:T(8,128)(2,1)} %param.26) | copy-start | bytes 49156
  7.1 0.7 %copy-start.8 = (bf16[64,32]{0,1:T(8,128)(2,1)S(1)}, bf16[64,32]{0,1:T(8,128)(2,1)}, u32[]{:S(2)}) copy-start(bf16[64,32]{0,1:T(8,128)(2,1)} %param.20) | copy-start | bytes 12292
  7.8 0.7 %copy-start.9 = (s32[16,12]{1,0:T(8,128)S(1)}, s32[16,12]{1,0:T(8,128)}, u32[]{:S(2)}) copy-start(s32[16,12]{1,0:T(8,128)} %mid_list.1) | copy-start | bytes 2308
  8.5 0.7 %copy-start.10 = (bf16[64,32]{0,1:T(8,128)(2,1)S(1)}, bf16[64,32]{0,1:T(8,128)(2,1)}, u32[]{:S(2)}) copy-start(bf16[64,32]{0,1:T(8,128)(2,1)} %param.25) | copy-start | bytes 12292
  9.2 0.7 %copy-start.11 = (s32[32,12]{0,1:T(8,128)S(1)}, s32[32,12]{0,1:T(8,128)}, u32[]{:S(2)}) copy-start(s32[32,12]{0,1:T(8,128)} %param.28) | copy-start | bytes 4612

commit v3 on v2

--- a/solution.py
+++ b/solution.py
@@ -120,14 +120,24 @@
 
 
 def kernel(
-    nb, nd,
-    fine_hbm, fine_list, fine_slot, fine_tr, theta_f, phi_f, mid_phase,
-    mid_list, mid_slot, mid_tr, theta_m, phi_m, coarse_phase, coarse_list, coarse_tr,
+    nb, nd, fine_hbm, *refs,
+):
+    smalls, refs = refs[:14], refs[14:]
+    held_smalls, refs = refs[-15:-1], refs[:-15] + refs[-1:]
+    climb(nb, nd, fine_hbm, smalls, held_smalls, *refs)
+
+
+def climb(
+    nb, nd, fine_hbm, smalls, held_smalls,
     fine_in, mid_in, coarse_in,
     fpad, par, mrecv, crs, crecv, along1, lift1, along2, lift2,
     cosm, sinm, cosc, sinc, fine_mask, mid_mask, coarse_mask, fine_wide, mid_wide, coarse_wide,
-    load_sem, fsend, frecv, msend, mrecv_sem, csend, crecv_sem,
+    load_sem, fsend, frecv, msend, mrecv_sem, csend, crecv_sem, small_sems,
 ):
+    (
+        fine_list, fine_slot, fine_tr, theta_f, phi_f, mid_phase,
+        mid_list, mid_slot, mid_tr, theta_m, phi_m, coarse_phase, coarse_list, coarse_tr,
+    ) = held_smalls
     n = nb * nd
     b, d = lax.axis_index("box"), lax.axis_index("dir")
     me = b * nd + d
@@ -144,6 +154,12 @@
 
     fine_load = pltpu.make_async_copy(fine_hbm, fpad.at[pl.ds(4, held)], load_sem)
     fine_load.start()
+    small_loads = [
+        pltpu.make_async_copy(source, place, small_sems.at[i])
+        for i, (source, place) in enumerate(zip(smalls, held_smalls))
+    ]
+    for load in small_loads:
+        load.start()
     barrier = pltpu.get_barrier_semaphore()
 
     def greet(j, _):
@@ -153,6 +169,8 @@
         return 0
 
     lax.fori_loop(0, n - 1, greet, 0)
+    for load in small_loads:
+        load.wait()
 
     bd1 = phi_blocks(phi_f[...], 2)
     k1 = kron_identity(theta_f[...], 16)
@@ -503,7 +521,12 @@
     slots = fine_list.shape[1]
     ctiles = max(1, width // LANES)
     vmem = pl.BlockSpec(memory_space=pltpu.VMEM)
-    smem = pl.BlockSpec(memory_space=pltpu.SMEM)
+    hbm = pl.BlockSpec(memory_space=pltpu.HBM)
+    smalls = (
+        fine_list, fine_slot, fine_translator, theta_up_fine.T, phi_up_fine.T, mid_phase,
+        middle_list, middle_slot, middle_translator, theta_up_middle.T, phi_up_middle.T, co_phase,
+        coarse_list.T, coarse_translator,
+    )
     dma = pltpu.SemaphoreType.DMA
     return pl.pallas_call(
         functools.partial(kernel, nb, nd),
@@ -512,10 +535,7 @@
             jax.ShapeDtypeStruct((middle_list.shape[0], comps, middle_translator.shape[2]), BF16),
             jax.ShapeDtypeStruct((coarse_list.shape[0], comps, width), BF16),
         ),
-        in_specs=[
-            pl.BlockSpec(memory_space=pl.ANY), vmem, smem, vmem, vmem, vmem, vmem,
-            vmem, smem, vmem, vmem, vmem, vmem, vmem, vmem,
-        ],
+        in_specs=[hbm] * (1 + len(smalls)),
         out_specs=(vmem, vmem, vmem),
         scratch_shapes=[
             pltpu.VMEM((held + 8, comps, fine_dirs), BF16),
@@ -538,18 +558,18 @@
             pltpu.VMEM((slots, 2, 8, middle_translator.shape[2]), F32),
             pltpu.VMEM((slots, 2, 8, width), F32),
             dma, dma((2,)), dma((2,)), dma((2 * nd,)), dma((nd + 2,)), dma((n,)), dma((n,)),
+            *[
+                (pltpu.SMEM if x.ndim == 1 else pltpu.VMEM)(x.shape, x.dtype) for x in smalls
+            ],
+            dma((len(smalls),)),
         ],
         compiler_params=pltpu.CompilerParams(
-            collective_id=0, has_side_effects=True, vmem_limit_bytes=48 * 1024 * 1024
+            collective_id=0, has_side_effects=True, vmem_limit_bytes=64 * 1024 * 1024
         ),
         cost_estimate=pl.CostEstimate(
             flops=4_000_000_000, bytes_accessed=4_000_000, transcendentals=0
         ),
-    )(
-        fine_out, fine_list, fine_slot, fine_translator, theta_up_fine.T, phi_up_fine.T, mid_phase,
-        middle_list, middle_slot, middle_translator, theta_up_middle.T, phi_up_middle.T, co_phase,
-        coarse_list.T, coarse_translator,
-    )
+    )(fine_out, *smalls)
 
 
 def solution(mesh):

time: 44.6 us -> 38 us (0.85)
  local copies, waits for them, and re-layouts: 11.6 us -> 3.97 us
  Pallas kernels: 31.6 us -> 33.1 us
    unnamed x33 -> x7, local copies, waits for them, and re-layouts: 11.6 us -> 3.97 us
    pallas_call x1, Pallas kernels: 31.6 us -> 33.1 us  [local(): pl.pallas_call(functools.partial(kernel, nb, nd), out_shape=(jax.ShapeDty...]
where the time goes in v3:
time: 38 us; the launch traced here: 37.7 us
  Pallas kernels  33.1 us (87%)
  local copies, waits for them, and re-layouts  3.97 us (10%)
  between operations  0.66 us (2%)
    pallas_call x1, Pallas kernels, local(): pl.pallas_call(functools.partial(kernel, nb, nd), out_shape=(jax.ShapeDty...  33.1 us
    unnamed x7, local copies, waits for them, and re-layouts  3.97 us

profile of v3, /device:TPU:11, one launch (start us, length us, event | category | flops | bytes accessed | tf_op | source)
XLA Modules:
  0.0 37.7 jit_solution(17362080088802379348)
XLA Ops:
  0.6 33.1 %shard_map.166 = (bf16[16,32,512]{2,1,0:T(8,128)(2,1)}, bf16[16,32,512]{2,1,0:T(8,128)(2,1)}, bf16[32,32,256]{2,1,0:T(8,128)(2,1)}) custom-call(bf16[16,32,512]{2,1,0:T(8,128)(2,1)} %fine_hbm.1, s32[16,12]{1,0:T(8,128)} %refs_0_.1, s32[64]{0:T(128)} %refs_1_.1, f32[12,2,512]{2,1,0:T(2,128)} %refs_2_.1, bf16[16,32]{1,0:T(8,128)(2,1)} %bitcast.17, ...), custom_call_target="tpu_custom_call" | custom-call | flops 4000000000 | bytes 4000000 | tf_op jit(solution)/shard_map/pallas_call | solution.py:531
  33.8 0.0 copy-start.1
  33.8 1.9 %copy.21 = bf16[16,32,512]{2,1,0:T(8,128)(2,1)} copy(bf16[16,32,512]{2,1,0:T(8,128)(2,1)} %get-tuple-element.6) | data formatting | bytes 1048576
  35.7 0.0 copy-done.1
  35.7 0.0 copy-start
  35.7 0.8 %copy.22 = bf16[16,32,512]{2,1,0:T(8,128)(2,1)} copy(bf16[16,32,512]{2,1,0:T(8,128)(2,1)S(1)} %copy-done.1) | data formatting | bytes 1048576
  36.5 0.4 %copy-done = bf16[32,32,256]{2,1,0:T(8,128)(2,1)S(1)} copy-done((bf16[32,32,256]{2,1,0:T(8,128)(2,1)S(1)}, bf16[32,32,256]{2,1,0:T(8,128)(2,1)}, u32[]{:S(2)}) %copy-start) | copy-done | bytes 524312
  37.0 0.8 %copy.23 = bf16[32,32,256]{2,1,0:T(8,128)(2,1)} copy(bf16[32,32,256]{2,1,0:T(8,128)(2,1)S(1)} %copy-done) | data formatting | bytes 1048576
Async XLA Ops:
  33.8 2.0 %copy-start.1 = (bf16[16,32,512]{2,1,0:T(8,128)(2,1)S(1)}, bf16[16,32,512]{2,1,0:T(8,128)(2,1)}, u32[]{:S(2)}) copy-start(bf16[16,32,512]{2,1,0:T(8,128)(2,1)} %get-tuple-element.7) | copy-start | bytes 1572868
  35.7 1.2 %copy-start = (bf16[32,32,256]{2,1,0:T(8,128)(2,1)S(1)}, bf16[32,32,256]{2,1,0:T(8,128)(2,1)}, u32[]{:S(2)}) copy-start(bf16[32,32,256]{2,1,0:T(8,128)(2,1)} %get-tuple-element.8) | copy-start | bytes 1572868
